TPU v7x, 128 devices: a whole 4x4x4 slice. The times are simulated.
128 devices in a mesh: col: 64 (over x, z, y), pw: 2 (over core).
Axes of the slice: x: 4, y: 4, z: 4, core: 2. Of those that a mesh axis runs over, the one named last changes fastest.
Arguments:
- exchange_pairs: bfloat16 [4096, 57344], P('pw', 'col'), may hold values from -0.046875 to 0.046875
- direct_pairs: bfloat16 [4096, 57344], P('pw', 'col'), may hold values from -0.046875 to 0.046875
- test_matrix: bfloat16 [57344, 256], P('col'), may hold values from -6 to 6
- energies: float32 [57344], P('col'), may hold values from 0.8 to 37.5
- picks: int32 [64, 32], P('col'), may hold values from 0 to 895, as said below
Outputs:
- sketch: float32 [2048, 256], P(('col', 'pw'))
- basis: float32 [2048, 256], P(('col', 'pw'))
- factor: float32 [256, 256], replicated
- gram: float32 [256, 256], replicated
Inputs may be any that keep to these rules, and one draw needn't show every extreme that they name: `picks`: each row lists 32 distinct local indices of one column block; 0 and 895 are among them.
All inputs are finite; a program needn't handle non-finite values.
Results may differ from a plain program's by a relative error of at most 0.00075.
Values may be sent and summed in bfloat16 or wider, within the bound.
No kernel may reach another device: no remote copies, remote signals or barrier semaphores. Data moves between devices by JAX's collectives and lax.ppermute only.
A program may use at most 128 MiB of HBM per device.

v0:
```python
import jax
import jax.numpy as jnp
from jax import lax
from jax.sharding import PartitionSpec as P


def contract_lead(left, right, highest):
    if highest:
        return lax.dot_general(
            left,
            right,
            (((0,), (0,)), ((), ())),
            precision=lax.Precision.HIGHEST,
            preferred_element_type=jnp.float32,
        )
    return lax.dot_general(
        left, right, (((0,), (0,)), ((), ())), preferred_element_type=jnp.float32
    )


def right_solve(lower, matrix):
    return lax.linalg.triangular_solve(lower, matrix, left_side=False, lower=True, transpose_a=True)


def shards(exchange_pairs, direct_pairs, test_matrix, energies, picks):
    local_rows = picks[0]
    row_count = local_rows.shape[0]
    half = row_count // 2
    lane = lax.axis_index("pw")
    own_x = jnp.take(exchange_pairs, local_rows, axis=1)
    own_y = jnp.take(direct_pairs, local_rows, axis=1)
    own_test = jnp.take(test_matrix, local_rows, axis=0).astype(jnp.float32)
    own_diag = jnp.take(energies, local_rows)[:, None] * own_test
    own_diag = lax.dynamic_slice_in_dim(own_diag, lane * half, half, 0)
    test_wide = test_matrix.astype(jnp.float32)
    stacked = jnp.stack([own_x, own_y])
    piece = lax.all_gather(stacked, "col", axis=2, tiled=True)
    kernel = 2.0 * contract_lead(piece[0], exchange_pairs, False)
    kernel = kernel - contract_lead(piece[1], direct_pairs, False)
    partial_rows = jnp.dot(kernel, test_wide, precision=lax.Precision.HIGHEST)
    mine = lax.psum_scatter(partial_rows, ("col", "pw"), scatter_dimension=0, tiled=True)
    sketch = mine + own_diag
    gram1 = lax.psum(contract_lead(sketch, sketch, True), ("col", "pw"))
    lower1 = jnp.linalg.cholesky(gram1)
    first = right_solve(lower1, sketch)
    gram2 = lax.psum(contract_lead(first, first, True), ("col", "pw"))
    lower2 = jnp.linalg.cholesky(gram2)
    second = right_solve(lower2, first)
    total_rows = jnp.float32(row_count * lax.axis_size("col"))
    scale = jnp.sqrt(total_rows)
    basis = second * scale
    factor = jnp.dot(lower2.T, lower1.T, precision=lax.Precision.HIGHEST) / scale
    gram = gram1 / total_rows
    return (sketch, basis, factor, gram)


def solution(mesh):
    return jax.shard_map(
        shards,
        mesh=mesh,
        in_specs=(P("pw", "col"), P("pw", "col"), P("col", None), P("col"), P("col", None)),
        out_specs=(P(("col", "pw"), None), P(("col", "pw"), None), P(), P()),
        check_vma=False,
    )
```

profile of v0, /device:TPU:1, one launch (start us, length us, event | category | flops | bytes accessed | tf_op | source)
XLA Modules:
  0.0 1222.7 jit_solution(14582846426217889902)
XLA Ops:
  7.2 0.7 fusion.39
  7.9 0.7 compare_select_fusion
  8.6 1.4 gather_fusion
  10.0 0.7 broadcast_select_fusion
  10.7 6.2 copy.16
  16.8 6.1 copy.17
  23.0 3.3 gather_fusion.2
  26.2 3.3 gather_fusion.3
  29.5 0.1 select_bitcast_fusion.1
  29.6 0.7 pad_maximum_fusion
  30.4 0.6 reduce-scatter.2.cloned.1.call-start
  31.0 107.2 %all-gather.2.cloned.1.call-done = bf16[2,2048,2048]{1,2,0:T(8,128)(2,1)} async-done(((bf16[2,2048,32]{1,2,0:T(8,128)(2,1)}), bf16[2,2048,2048]{1,2,0:T(8,128)(2,1)}) %all-gather.2.cloned.1.call-update) | async-done | bytes 16777232 | tf_op jit(solution)/shard_map/all_gather | solution.py:37
  138.1 12.4 %fusion = f32[2048,896]{1,0:T(8,128)S(1)} fusion(bf16[2048,896]{1,0:T(8,128)(2,1)} %param.11, bf16[2,2048,2048]{1,2,0:T(8,128)(2,1)} %all-gather.2.cloned.1.call-done), kind=kOutput, calls=%fused_computation.9 | convolution fusion | flops 7516192768 | bytes 19398656 | tf_op jit(solution)/shard_map/dot_general | solution.py:16
  150.6 11.2 fusion.1
  161.8 5.6 fusion.2
  167.5 0.6 gather_fusion.1
  168.1 0.1 dynamic-slice.5
  168.2 0.1 dynamic-slice.6
  168.3 631.7 %reduce-scatter.2.cloned.1.call-done = f32[16,256]{1,0:T(8,128)} async-done(((f32[2048,256]{1,0:T(8,128)}), f32[16,256]{1,0:T(8,128)}) %reduce-scatter.2.cloned.1.call-update) | async-done | bytes 16400 | tf_op jit(solution)/shard_map/reduce_scatter | solution.py:41
  800.0 0.8 multiply_add_fusion
  800.8 1.1 fusion.47
  801.9 0.2 all-reduce.6.cloned.1.call-start
  802.1 145.9 %all-reduce.4.cloned.1.call-done = f32[256,256]{0,1:T(8,128)} async-done(((f32[256,256]{0,1:T(8,128)}), f32[256,256]{0,1:T(8,128)}) %all-reduce.4.cloned.1.call-update) | async-done | bytes 262160 | tf_op jit(solution)/shard_map/psum | solution.py:43
  948.1 1.1 copy.19
  949.2 1.0 fusion.7
  950.2 11.7 cholesky.130
  961.9 9.8 custom-call.13
  971.8 0.2 constant_dynamic-update-slice_fusion.3
  972.0 0.3 convolution_subtract_fusion.1
  972.2 11.7 cholesky.147
  984.0 0.7 compare_reduce_fusion.2
  986.1 4.0 while.4
  986.1 0.6 fusion.63
  986.7 1.4 bitcast_dynamic-update-slice_fusion.4
  988.1 0.6 fusion.63
  988.7 1.4 bitcast_dynamic-update-slice_fusion.4
  990.0 19.9 %custom-call.14 = f32[2,128,128]{1,2,0:T(8,128)S(1)} custom-call(f32[2,128,128]{2,1,0:T(8,128)S(1)} %get-tuple-element.21), custom_call_target="InvertDiagBlocksLowerTriangular" | custom-call | tf_op jit(solution)/shard_map/triangular_solve/custom-call.0 | solution.py:22
  1009.9 0.2 fusion.25
  1010.1 0.2 convolution_subtract_fusion.3
  1010.3 0.2 fusion.23
  1010.5 1.1 fusion.34
  1011.7 1.0 broadcast_multiply_fusion
  1012.6 0.8 copy.22
  1013.5 137.3 %all-reduce.6.cloned.1.call-done = f32[256,256]{0,1:T(8,128)} async-done(((f32[256,256]{0,1:T(8,128)}), f32[256,256]{0,1:T(8,128)}) %all-reduce.6.cloned.1.call-update) | async-done | bytes 262160 | tf_op jit(solution)/shard_map/psum | solution.py:46
  1150.8 1.1 copy.21
  1151.9 1.0 fusion.6
  1152.9 11.7 cholesky.164
  1164.7 9.8 custom-call.15
  1174.5 0.2 constant_dynamic-update-slice_fusion.1
  1174.7 0.3 convolution_subtract_fusion
  1175.0 11.7 cholesky.181
  1186.7 0.7 compare_reduce_fusion
  1187.4 0.6 compare_reduce_fusion.1
  1189.4 1.2 convolution_multiply_fusion
  1190.7 4.1 while.5
  1190.7 0.7 fusion.64
  1191.4 1.3 bitcast_dynamic-update-slice_fusion.5
  1192.7 0.7 fusion.64
  1193.4 1.3 bitcast_dynamic-update-slice_fusion.5
  1194.8 19.9 %custom-call.16 = f32[2,128,128]{1,2,0:T(8,128)S(1)} custom-call(f32[2,128,128]{2,1,0:T(8,128)S(1)} %get-tuple-element.22), custom_call_target="InvertDiagBlocksLowerTriangular" | custom-call | tf_op jit(solution)/shard_map/triangular_solve/custom-call.0 | solution.py:22
  1214.7 0.2 fusion.20
  1214.8 0.2 convolution_subtract_fusion.2
  1215.0 0.2 fusion.18
  1215.2 0.6 maximum_multiply_fusion
  (32 shorter events, 0.5 us)
Async XLA Ops:
  7.2 154.6 %copy-start = (bf16[896,256]{1,0:T(8,128)(2,1)S(1)}, bf16[896,256]{1,0:T(8,128)(2,1)}, u32[]{:S(2)}) copy-start(bf16[896,256]{1,0:T(8,128)(2,1)} %param.12) | copy-start | bytes 1376260
  7.2 130.9 %all-gather.2.cloned.1.call-start = ((), (), s32[]{:S(2)}) async-start(), calls=%async_computation.1 | async-start | bytes 17039360 | tf_op jit(solution)/shard_map/all_gather | solution.py:37
  30.4 769.6 %reduce-scatter.2.cloned.1.call-start = ((), (), s32[]{:S(2)}) async-start(), calls=%async_computation.2 | async-start | bytes 2113536 | tf_op jit(solution)/shard_map/reduce_scatter | solution.py:41
  138.1 12.4 %copy-start.1 = (bf16[2048,896]{1,0:T(8,128)(2,1)S(1)}, bf16[2048,896]{1,0:T(8,128)(2,1)}, u32[]{:S(2)}) copy-start(bf16[2048,896]{1,0:T(8,128)(2,1)} %param.10) | copy-start | bytes 11010052
  167.4 780.7 %all-reduce.4.cloned.1.call-start = ((), (), s32[]{:S(2)}) async-start(), calls=%async_computation.3 | async-start | bytes 524288 | tf_op jit(solution)/shard_map/psum | solution.py:43
  800.8 415.1 %copy-start.2 = (f32[16,256]{1,0:T(8,128)}, f32[16,256]{1,0:T(8,128)S(1)}, u32[]{:S(2)}) copy-start(f32[16,256]{1,0:T(8,128)S(1)} %multiply_add_fusion) | copy-start | bytes 49156
  801.9 348.9 %all-reduce.6.cloned.1.call-start = ((), (), s32[]{:S(2)}) async-start(), calls=%async_computation.4 | async-start | bytes 524288 | tf_op jit(solution)/shard_map/psum | solution.py:46
Sparse Core Ops, SparseCore 0:
  30.5 107.5 all-gather.1
  167.5 632.3 reduce-scatter.1
  806.0 142.0 all-reduce.3
  1011.8 138.9 all-reduce.5
where the time goes:
time: 1230 us; the launch traced here: 1220 us
  waiting for transfers between devices  1020 us (83%)
  other arithmetic  116 us (9%)
  matrix products  34.7 us (3%)
  local copies, waits for them, and re-layouts  32.1 us (3%)
  between operations  16.9 us (1%)
    reduce_scatter x1, waiting for transfers between devices, shards(): lax.psum_scatter(partial_rows, ('col', 'pw'), scatter_dimension=0, tiled=...  632 us
    psum x1, waiting for transfers between devices, shards(): gram1 = lax.psum(contract_lead(sketch, sketch, True), ('col', 'pw'))  146 us
    psum x1, waiting for transfers between devices, shards(): gram2 = lax.psum(contract_lead(first, first, True), ('col', 'pw'))  137 us
    all_gather x1, waiting for transfers between devices, shards(): piece = lax.all_gather(stacked, 'col', axis=2, tiled=True)  107 us
    another operation x5, other arithmetic, right_solve(): lax.linalg.triangular_solve(lower, matrix, left_side=False, lower=True, t...  39.9 us
    another operation x7, other arithmetic, shards(): lower2 = jnp.linalg.cholesky(gram2)  34.7 us
    another operation x6, other arithmetic, shards(): lower1 = jnp.linalg.cholesky(gram1)  34 us
  transfers between devices with their start and end apart: 4, of which 4 were waited for; matrix products, arithmetic and copies ran while one was open for 0% of the time, Pallas kernels for 0%

commit v1 on v0

v1 whole, which is shorter than its diff:
```python
import jax
import jax.numpy as jnp
from jax import lax
from jax.experimental import pallas as pl
from jax.experimental.pallas import tpu as pltpu
from jax.sharding import PartitionSpec as P

HIGH = lax.Precision.HIGHEST
F32 = jnp.float32


def dot_lead(left, right):
    return lax.dot_general(left, right, (((0,), (0,)), ((), ())), precision=HIGH, preferred_element_type=F32)


def dot_last(left, right):
    return lax.dot_general(left, right, (((1,), (1,)), ((), ())), precision=HIGH, preferred_element_type=F32)


def splat_lane(tile, lane):
    return jnp.broadcast_to(tile[:, lane:lane + 1], (8, 128))


def splat_row(tile, row):
    return jnp.broadcast_to(tile[row:row + 1, :], (8, 128))


def factor_inverse(work, upper, outer):
    n = work.shape[0]
    tiles = n // 128
    sub = lax.broadcasted_iota(jnp.int32, (8, 128), 0)
    lane = lax.broadcasted_iota(jnp.int32, (8, 128), 1)
    for r0 in range(0, n, outer):
        count = outer // 8
        panel = [[work[r0 + 8 * t:r0 + 8 * t + 8, 128 * c:128 * c + 128] for c in range(tiles)] for t in range(count)]
        for b in range(count):
            r = r0 + 8 * b
            own, base = r // 128, r % 128
            cols = {t: [splat_lane(panel[t][own], base + j) for j in range(8)] for t in range(b, count)}
            d = [[splat_row(cols[b][j], i) if i >= j else None for j in range(8)] for i in range(8)]
            inv = [None] * 8
            low = [[None] * 8 for _ in range(8)]
            for j in range(8):
                inv[j] = lax.rsqrt(d[j][j])
                for i in range(j + 1, 8):
                    low[i][j] = d[i][j] * inv[j]
                for i in range(j + 1, 8):
                    for k in range(j + 1, i + 1):
                        d[i][k] = d[i][k] - low[i][j] * low[k][j]
            mine = (lane >= base) & (lane < base + 8)
            cleared = jnp.where(mine, jnp.where(lane - base == sub, 1.0, 0.0), panel[b][own])
            sources = [panel[b][c] if c != own else cleared for c in range(tiles)] + [panel[b][own]]
            rows = [[splat_row(src, j) for src in sources] for j in range(8)]
            for j in range(8):
                for s in range(tiles + 1):
                    acc = rows[j][s]
                    for k in range(j):
                        acc = acc - low[j][k] * rows[k][s]
                    rows[j][s] = acc * inv[j]
            done = []
            for s in range(tiles + 1):
                tile = rows[0][s]
                for j in range(1, 8):
                    tile = jnp.where(sub == j, rows[j][s], tile)
                done.append(tile)
            for c in range(tiles):
                work[r:r + 8, 128 * c:128 * c + 128] = done[c]
                if c < own:
                    upper[r:r + 8, 128 * c:128 * c + 128] = jnp.zeros((8, 128), F32)
                elif c == own:
                    upper[r:r + 8, 128 * c:128 * c + 128] = jnp.where(lane >= base + sub, done[tiles], 0.0)
                else:
                    upper[r:r + 8, 128 * c:128 * c + 128] = done[c]
            for t in range(b + 1, count):
                below = []
                for j in range(8):
                    acc = cols[t][j]
                    for k in range(j):
                        acc = acc - below[k] * low[j][k]
                    below.append(acc * inv[j])
                for c in range(tiles):
                    acc = panel[t][c]
                    if c == own:
                        acc = jnp.where(mine, 0.0, acc)
                    for j in range(8):
                        acc = acc - below[j] * rows[j][c]
                    panel[t][c] = acc
        after = r0 + outer
        if after < n:
            first_lane = after // 128 * 128
            left = upper[r0:after, first_lane:n]
            done_col = lax.broadcasted_iota(jnp.int32, (outer, n), 1)
            done_row = lax.broadcasted_iota(jnp.int32, (outer, n), 0) + r0
            right = jnp.where((done_col > done_row) & (done_col < after), 0.0, work[r0:after, :])
            change = dot_lead(left, right)
            col = lax.broadcasted_iota(jnp.int32, (n - after, n), 1)
            rest = jnp.where((col >= r0) & (col < after), 0.0, work[after:n, :])
            work[after:n, :] = rest - change[after - first_lane:, :]


def tail_kernel(where_ref, mine_ref, other_ref, basis_ref, factor_ref, gram_ref, held, work, upper, first_upper):
    n = work.shape[0]
    rows = basis_ref.shape[0]
    part = mine_ref.shape[0]
    total = float(2 * part)
    lane = where_ref[0]
    held[pl.ds(pl.multiple_of(lane * part, part), part), :] = mine_ref[...]
    held[pl.ds(pl.multiple_of((1 - lane) * part, part), part), :] = other_ref[...]
    row = lax.broadcasted_iota(jnp.int32, (n, n), 0)
    col = lax.broadcasted_iota(jnp.int32, (n, n), 1)
    gram1 = dot_lead(held[...], held[...])
    gram_ref[...] = gram1 / total
    work[...] = gram1

    def one_pass(step, _):
        factor_inverse(work, upper, 64)
        inverse = jnp.where(col <= row, work[...], 0.0)

        @pl.when(step == 0)
        def _():
            first_upper[...] = upper[...]
            first = dot_last(held[...], inverse)
            held[...] = first
            work[...] = dot_lead(first, first)

        @pl.when(step == 1)
        def _():
            at = pl.multiple_of(where_ref[1], 16)
            basis_ref[...] = dot_last(held[pl.ds(at, rows), :], inverse) * (total ** 0.5)
            factor_ref[...] = jnp.dot(upper[...], first_upper[...], precision=HIGH, preferred_element_type=F32) / (total ** 0.5)

        return 0

    lax.fori_loop(0, 2, one_pass, 0)


def tail(mine, other, where, rows):
    part, n = mine.shape
    vmem = pl.BlockSpec(memory_space=pltpu.VMEM)
    return pl.pallas_call(
        tail_kernel,
        out_shape=(
            jax.ShapeDtypeStruct((rows, n), F32),
            jax.ShapeDtypeStruct((n, n), F32),
            jax.ShapeDtypeStruct((n, n), F32),
        ),
        in_specs=[pl.BlockSpec(memory_space=pltpu.SMEM), vmem, vmem],
        out_specs=(vmem, vmem, vmem),
        scratch_shapes=[
            pltpu.VMEM((2 * part, n), F32),
            pltpu.VMEM((n, n), F32),
            pltpu.VMEM((n, n), F32),
            pltpu.VMEM((n, n), F32),
        ],
        compiler_params=pltpu.CompilerParams(vmem_limit_bytes=48 * 1024 * 1024),
    )(where, mine, other)


def first_kernel(picks_row, picks_col, energy_row, test, left_x, left_y, packed, diagonal, chosen):
    width = test.shape[0]
    block = left_x.shape[0]
    cells = packed.shape[0]
    part = block // cells
    count = picks_col.shape[0]

    @pl.when(pl.program_id(0) == 0)
    def _():
        spot = lax.broadcasted_iota(jnp.int32, (width, 128), 0) == picks_row[...]
        chosen[...] = jnp.where(spot, 1.0, 0.0).astype(jnp.bfloat16)
        here = lax.broadcasted_iota(jnp.int32, (count, width), 1) == picks_col[...]
        energy = jnp.sum(jnp.where(here, energy_row[...], 0.0), axis=1, keepdims=True)
        taken = lax.dot_general(
            here.astype(F32).astype(jnp.bfloat16), test[...], (((1,), (0,)), ((), ())), preferred_element_type=F32
        )
        diagonal[...] = energy * taken

    right = test[...]
    own = []
    for at, (left, weight) in enumerate(((left_x, 2.0), (left_y, -1.0))):
        image = jnp.dot(left[...], right, preferred_element_type=F32) * weight
        packed[:, at * part:(at + 1) * part, :] = image.reshape(cells, part, image.shape[1])
        own.append(jnp.dot(left[...], chosen[...], preferred_element_type=F32).T)
    for cell in range(cells):
        pieces = []
        for group in range(count // 8):
            for rows in own:
                pieces.append(rows[8 * group:8 * group + 8, cell * part:(cell + 1) * part])
        packed[cell, 2 * part:2 * part + 8, :] = jnp.concatenate(pieces, axis=1)


def first_call(exchange, direct, test, energies, picks, cells):
    depth, width = exchange.shape
    rank = test.shape[1]
    count = picks.shape[1]
    part = depth // cells
    block = 256
    per = block // part
    picks_row = jnp.pad(picks, ((0, 0), (0, 128 - count)), constant_values=-1)
    whole = lambda *shape: pl.BlockSpec(shape, lambda i: (0,) * len(shape))
    return pl.pallas_call(
        first_kernel,
        grid=(depth // block,),
        in_specs=[
            whole(1, 128),
            whole(count, 1),
            whole(1, width),
            whole(width, rank),
            pl.BlockSpec((block, width), lambda i: (i, 0)),
            pl.BlockSpec((block, width), lambda i: (i, 0)),
        ],
        out_specs=(
            pl.BlockSpec((per, 2 * part + 8, rank), lambda i: (i, 0, 0)),
            whole(count, rank),
        ),
        out_shape=(
            jax.ShapeDtypeStruct((cells, 2 * part + 8, rank), F32),
            jax.ShapeDtypeStruct((count, rank), F32),
        ),
        scratch_shapes=[pltpu.VMEM((width, 128), jnp.bfloat16)],
        compiler_params=pltpu.CompilerParams(vmem_limit_bytes=32 * 1024 * 1024),
    )(picks_row, picks.reshape(count, 1), energies.reshape(1, width), test, exchange, direct)


def split3(value):
    high = value.astype(jnp.bfloat16)
    rest = value - high.astype(F32)
    middle = rest.astype(jnp.bfloat16)
    low = (rest - middle.astype(F32)).astype(jnp.bfloat16)
    return high, middle, low


def couple_kernel(lane_ref, packed, keep, give):
    cells, height, rank = packed.shape
    depth = height - 8
    image = packed[0, :depth, :]
    for cell in range(1, cells):
        image = image + packed[cell, :depth, :]
    parts = split3(image)
    rows = packed[:, depth:, :].reshape(cells * 8, rank).astype(jnp.bfloat16)
    lane = lane_ref[0]
    for group in range(rank // depth):
        left = rows[:, group * depth:(group + 1) * depth]
        out = jnp.zeros((cells * 8, rank), F32)
        for piece in reversed(parts):
            out = out + jnp.dot(left, piece, preferred_element_type=F32)
        out = out.reshape(cells, 8, rank)
        half, at = group // 2, group % 2 * 8

        @pl.when(lane == half)
        def _():
            keep[:, at:at + 8, :] = out

        @pl.when(lane != half)
        def _():
            give[:, at:at + 8, :] = out


def couple(lane, packed):
    cells, height, rank = packed.shape
    vmem = pl.BlockSpec(memory_space=pltpu.VMEM)
    shape = jax.ShapeDtypeStruct((cells, 16, rank), F32)
    return pl.pallas_call(
        couple_kernel,
        out_shape=(shape, shape),
        in_specs=[pl.BlockSpec(memory_space=pltpu.SMEM), vmem],
        out_specs=(vmem, vmem),
        compiler_params=pltpu.CompilerParams(vmem_limit_bytes=40 * 1024 * 1024),
    )(lane, packed)


SWAP = [(0, 1), (1, 0)]


def shards(exchange_pairs, direct_pairs, test_matrix, energies, picks):
    cells = lax.axis_size("col")
    lane = lax.axis_index("pw")
    place = lax.axis_index("col")
    lane_ref = lane.astype(jnp.int32).reshape(1)
    packed, diagonal = first_call(exchange_pairs, direct_pairs, test_matrix, energies, picks, cells)
    packed = lax.all_to_all(packed, "col", split_axis=0, concat_axis=0, tiled=True)
    keep, give = couple(lane_ref, packed)
    both = keep + lax.ppermute(give, "pw", SWAP)
    arrived = lax.all_to_all(both, "col", split_axis=0, concat_axis=0, tiled=True)
    half = both.shape[1]
    sketch = jnp.sum(arrived, axis=0) + lax.dynamic_slice_in_dim(diagonal, lane * half, half, 0)
    copies = jnp.broadcast_to(sketch[None], (cells,) + sketch.shape)
    mine = lax.all_to_all(copies, "col", split_axis=0, concat_axis=0, tiled=True)
    other = lax.ppermute(mine, "pw", SWAP)
    where = jnp.stack([lane, lane * (cells * half) + place * half]).astype(jnp.int32)
    rank = sketch.shape[1]
    basis, factor, gram = tail(mine.reshape(cells * half, rank), other.reshape(cells * half, rank), where, half)
    return (sketch, basis, factor, gram)


def solution(mesh):
    return jax.shard_map(
        shards,
        mesh=mesh,
        in_specs=(P("pw", "col"), P("pw", "col"), P("col", None), P("col"), P("col", None)),
        out_specs=(P(("col", "pw"), None), P(("col", "pw"), None), P(), P()),
        check_vma=False,
    )
```

time: 1230 us -> 187 us (0.15)
  waiting for transfers between devices: 1020 us -> 79.1 us
  other arithmetic: 116 us -> 1.36 us
  Pallas kernels: 0 us -> 39.8 us
  matrix products: 34.7 us -> 0 us
  starting transfers between devices: 0.86 us -> 34.2 us
  local copies, waits for them, and re-layouts: 32.1 us -> 9.48 us
  blocking collectives: 0 us -> 21.6 us
  between operations: 16.9 us -> 0.71 us
    reduce_scatter x1 -> x0, waiting for transfers between devices: 632 us -> none  [shards(): lax.psum_scatter(partial_rows, ('col', 'pw'), scatter_dimension=0, tiled=...]
    psum x2 -> x0, waiting for transfers between devices: 283 us -> none  [the longest x1 146 us: shards(): gram1 = lax.psum(contract_lead(sketch, sketch, True), ('col', 'pw'))]
    another operation x20 -> x1, other arithmetic: 109 us -> 0.07 us  [shards(): jnp.stack([lane, lane * (cells * half) + place * half]).astype(jnp.int32)]
    all_gather x1 -> x0, waiting for transfers between devices: 107 us -> none  [shards(): piece = lax.all_gather(stacked, 'col', axis=2, tiled=True)]
    all_to_all x0 -> x2, waiting for transfers between devices: none -> 74.6 us  [the longest x1 57.6 us: shards(): lax.all_to_all(packed, 'col', split_axis=0, concat_axis=0, tiled=True)]
    pallas_call x0 -> x3, Pallas kernels: none -> 39.8 us  [the longest x1 28.1 us: tail(): pl.pallas_call(tail_kernel, out_shape=(jax.ShapeDtypeStruct((rows, n), F3...]
    dot_general x6 -> x0, matrix products: 32.7 us -> none  [the longest x2 23.6 us: contract_lead(): lax.dot_general(left, right, (((0,), (0,)), ((), ())), preferred_element_...]
    all_to_all x0 -> x2, starting transfers between devices: none -> 27.1 us  [the longest x1 14.9 us: shards(): lax.all_to_all(both, 'col', split_axis=0, concat_axis=0, tiled=True)]
where the time goes in v1:
time: 187 us; the launch traced here: 186 us
  waiting for transfers between devices  79.1 us (42%)
  Pallas kernels  39.8 us (21%)
  starting transfers between devices  34.2 us (18%)
  blocking collectives  21.6 us (12%)
  local copies, waits for them, and re-layouts  9.48 us (5%)
    all_to_all x1, waiting for transfers between devices, shards(): lax.all_to_all(packed, 'col', split_axis=0, concat_axis=0, tiled=True)  57.6 us
    pallas_call x1, Pallas kernels, tail(): pl.pallas_call(tail_kernel, out_shape=(jax.ShapeDtypeStruct((rows, n), F3...  28.1 us
    all_to_all x1, blocking collectives, shards(): lax.all_to_all(copies, 'col', split_axis=0, concat_axis=0, tiled=True)  21.6 us
    all_to_all x1, waiting for transfers between devices, shards(): lax.all_to_all(both, 'col', split_axis=0, concat_axis=0, tiled=True)  17 us
    all_to_all x1, starting transfers between devices, shards(): lax.all_to_all(both, 'col', split_axis=0, concat_axis=0, tiled=True)  14.9 us
    all_to_all x1, starting transfers between devices, shards(): lax.all_to_all(packed, 'col', split_axis=0, concat_axis=0, tiled=True)  12.2 us
    unnamed x10, local copies, waits for them, and re-layouts  7.28 us
    pallas_call x1, Pallas kernels, first_call(): pl.pallas_call(first_kernel, grid=(depth // block,), in_specs=[whole(1, 1...  6.77 us
  transfers between devices with their start and end apart: 4, of which 4 were waited for; matrix products, arithmetic and copies ran while one was open for 0% of the time, Pallas kernels for 0%

profile of v1, /device:TPU:1, one launch (start us, length us, event | category | flops | bytes accessed | tf_op | source)
XLA Modules:
  0.0 186.4 jit_solution(6186170730020473083)
XLA Ops:
  0.6 0.7 pad.4.picks_row
  1.3 0.7 copy.9.picks_col
  2.0 0.7 reshape.26.energy_row
  2.7 0.0 copy-start.1
  2.7 2.0 %copy-done.1 = bf16[2048,896]{1,0:T(8,128)(2,1)S(1)} copy-done((bf16[2048,896]{1,0:T(8,128)(2,1)S(1)}, bf16[2048,896]{1,0:T(8,128)(2,1)}, u32[]{:S(2)}) %copy-start.1) | copy-done | bytes 3670040
  4.8 0.0 copy-start.2
  4.8 2.0 %copy-done.2 = bf16[2048,896]{1,0:T(8,128)(2,1)S(1)} copy-done((bf16[2048,896]{1,0:T(8,128)(2,1)S(1)}, bf16[2048,896]{1,0:T(8,128)(2,1)}, u32[]{:S(2)}) %copy-start.2) | copy-done | bytes 3670040
  6.8 0.0 copy-start.3
  6.8 1.0 copy-done.3
  7.8 6.8 %shard_map.84 = (f32[64,72,256]{2,1,0:T(8,128)S(1)}, f32[32,256]{1,0:T(8,128)S(1)}) custom-call(s32[1,128]{1,0:T(1,128)S(1)} %pad.4.picks_row, s32[32,1]{1,0:T(8,128)S(1)} %copy.9.picks_col, f32[1,896]{1,0:T(1,128)S(1)} %reshape.26.energy_row, bf16[896,256]{1,0:T(8,128)(2,1)S(1)} %copy-done.3, bf16[2048,896]{1,0:T(8,128)(2,1)S(1)} %copy-done.1, ...), custom_call_target="tpu_custom_call" | custom-call | tf_op jit(solution)/shard_map/pallas_call | solution.py:200
  14.6 0.0 copy-start
  14.6 2.2 %copy-done = f32[64,72,256]{2,1,0:T(8,128)} copy-done((f32[64,72,256]{2,1,0:T(8,128)}, f32[64,72,256]{2,1,0:T(8,128)S(1)}, u32[]{:S(2)}) %copy-start) | copy-done | bytes 4718616
  16.8 12.2 %all-to-all-start = ((f32[64,72,256]{2,1,0:T(8,128)}), f32[64,72,256]{2,1,0:T(8,128)}, u32[]{:S(2)}, u32[]{:S(2)}) async-start(f32[64,72,256]{2,1,0:T(8,128)} %copy-done), calls=%async_computation | async-start | bytes 9437184 | tf_op jit(solution)/shard_map/all_to_all | solution.py:280
  29.0 57.6 %all-to-all-done.packed = f32[64,72,256]{2,1,0:T(8,128)} async-done(((f32[64,72,256]{2,1,0:T(8,128)}), f32[64,72,256]{2,1,0:T(8,128)}, u32[]{:S(2)}, u32[]{:S(2)}) %all-to-all-start) | async-done | bytes 4718624 | tf_op jit(solution)/shard_map/all_to_all | solution.py:280
  86.6 4.9 %shard_map.85 = (f32[64,16,256]{2,1,0:T(8,128)S(1)}, f32[64,16,256]{2,1,0:T(8,128)S(1)}) custom-call(s32[1]{0:T(128)} %bitcast.lane_ref, f32[64,72,256]{2,1,0:T(8,128)} %all-to-all-done.packed), custom_call_target="tpu_custom_call" | custom-call | tf_op jit(solution)/shard_map/pallas_call | solution.py:262
  91.5 3.9 %collective-permute-start = (f32[64,16,256]{2,1,0:T(8,128)S(1)}, f32[64,16,256]{2,1,0:T(8,128)S(1)}, u32[]{:S(2)}, u32[]{:S(2)}) collective-permute-start(f32[64,16,256]{2,1,0:T(8,128)S(1)} %get-tuple-element.13), channel_id=1, source_target_pairs={{0,1},{1,0},{2,3},{3,2},{4,5},{5,4},{6,7},{7,6},{8,9},{9,8},{10,11... | collective-permute-start | bytes 3145736 | tf_op jit(solution)/shard_map/ppermute | solution.py:282
  95.4 2.3 %collective-permute-done = f32[64,16,256]{2,1,0:T(8,128)S(1)} collective-permute-done((f32[64,16,256]{2,1,0:T(8,128)S(1)}, f32[64,16,256]{2,1,0:T(8,128)S(1)}, u32[]{:S(2)}, u32[]{:S(2)}) %collective-permute-start) | collective-permute-done | bytes 1048608 | tf_op jit(solution)/shard_map/ppermute | solution.py:282
  97.7 1.2 add.14
  98.9 14.9 %all-to-all-start.1 = ((f32[64,16,256]{2,1,0:T(8,128)}), f32[64,16,256]{2,1,0:T(8,128)S(1)}, u32[]{:S(2)}, u32[]{:S(2)}) async-start(f32[64,16,256]{2,1,0:T(8,128)} %add.14), calls=%async_computation.1 | async-start | bytes 2097152 | tf_op jit(solution)/shard_map/all_to_all | solution.py:283
  113.8 17.0 %all-to-all-done.1 = f32[64,16,256]{2,1,0:T(8,128)S(1)} async-done(((f32[64,16,256]{2,1,0:T(8,128)}), f32[64,16,256]{2,1,0:T(8,128)S(1)}, u32[]{:S(2)}, u32[]{:S(2)}) %all-to-all-start.1) | async-done | bytes 1048608 | tf_op jit(solution)/shard_map/all_to_all | solution.py:283
  130.8 0.1 reduce_sum.9
  130.9 0.0 copy-start.4
  130.9 0.1 broadcast_in_dim.2
  131.1 21.6 %all_to_all.15 = f32[64,16,256]{2,1,0:T(8,128)S(1)} all-to-all(f32[64,16,256]{2,1,0:T(8,128)S(1)} %broadcast_in_dim.2), channel_id=1, replica_groups=mesh['col'=64,'pw'=2] {'col'}, dimensions={0} | all-to-all | bytes 2097152 | tf_op jit(solution)/shard_map/all_to_all | solution.py:287
  152.7 3.3 %collective-permute-start.1 = (f32[64,16,256]{2,1,0:T(8,128)S(1)}, f32[64,16,256]{2,1,0:T(8,128)S(1)}, u32[]{:S(2)}, u32[]{:S(2)}) collective-permute-start(f32[64,16,256]{2,1,0:T(8,128)S(1)} %all_to_all.15), channel_id=1, source_target_pairs={{0,1},{1,0},{2,3},{3,2},{4,5},{5,4},{6,7},{7,6},{8,9},{9,8},{10,11... | collective-permute-start | bytes 3145736 | tf_op jit(solution)/shard_map/ppermute | solution.py:288
  156.0 0.1 pad_add_fusion.where_ref
  156.0 2.2 %collective-permute-done.1 = f32[64,16,256]{2,1,0:T(8,128)S(1)} collective-permute-done((f32[64,16,256]{2,1,0:T(8,128)S(1)}, f32[64,16,256]{2,1,0:T(8,128)S(1)}, u32[]{:S(2)}, u32[]{:S(2)}) %collective-permute-start.1) | collective-permute-done | bytes 1048608 | tf_op jit(solution)/shard_map/ppermute | solution.py:288
  158.3 28.1 %shard_map.86 = (f32[16,256]{1,0:T(8,128)}, f32[256,256]{1,0:T(8,128)}, f32[256,256]{1,0:T(8,128)}) custom-call(s32[2]{0:T(128)S(1)} %pad_add_fusion.where_ref, f32[1024,256]{1,0:T(8,128)S(1)} %bitcast.5, f32[1024,256]{1,0:T(8,128)S(1)} %bitcast.6), custom_call_target="tpu_custom_call" | custom-call | tf_op jit(solution)/shard_map/pallas_call | solution.py:140
  186.4 0.0 copy-done.4
  (1 shorter events, 0.0 us)
Async XLA Ops:
  2.7 2.0 %copy-start.1 = (bf16[2048,896]{1,0:T(8,128)(2,1)S(1)}, bf16[2048,896]{1,0:T(8,128)(2,1)}, u32[]{:S(2)}) copy-start(bf16[2048,896]{1,0:T(8,128)(2,1)} %left_x.1) | copy-start | bytes 11010052
  4.8 2.0 %copy-start.2 = (bf16[2048,896]{1,0:T(8,128)(2,1)S(1)}, bf16[2048,896]{1,0:T(8,128)(2,1)}, u32[]{:S(2)}) copy-start(bf16[2048,896]{1,0:T(8,128)(2,1)} %left_y.1) | copy-start | bytes 11010052
  6.8 1.0 copy-start.3
  14.6 2.2 %copy-start = (f32[64,72,256]{2,1,0:T(8,128)}, f32[64,72,256]{2,1,0:T(8,128)S(1)}, u32[]{:S(2)}) copy-start(f32[64,72,256]{2,1,0:T(8,128)S(1)} %get-tuple-element.11) | copy-start | bytes 14155780
  16.8 69.8 %all-to-all-start = ((f32[64,72,256]{2,1,0:T(8,128)}), f32[64,72,256]{2,1,0:T(8,128)}, u32[]{:S(2)}, u32[]{:S(2)}) async-start(f32[64,72,256]{2,1,0:T(8,128)} %copy-done), calls=%async_computation | async-start | bytes 9437184 | tf_op jit(solution)/shard_map/all_to_all | solution.py:280
  91.5 6.2 %collective-permute-start = (f32[64,16,256]{2,1,0:T(8,128)S(1)}, f32[64,16,256]{2,1,0:T(8,128)S(1)}, u32[]{:S(2)}, u32[]{:S(2)}) collective-permute-start(f32[64,16,256]{2,1,0:T(8,128)S(1)} %get-tuple-element.13), channel_id=1, source_target_pairs={{0,1},{1,0},{2,3},{3,2},{4,5},{5,4},{6,7},{7,6},{8,9},{9,8},{10,11... | collective-permute-start | bytes 3145736 | tf_op jit(solution)/shard_map/ppermute | solution.py:282
  98.9 31.9 %all-to-all-start.1 = ((f32[64,16,256]{2,1,0:T(8,128)}), f32[64,16,256]{2,1,0:T(8,128)S(1)}, u32[]{:S(2)}, u32[]{:S(2)}) async-start(f32[64,16,256]{2,1,0:T(8,128)} %add.14), calls=%async_computation.1 | async-start | bytes 2097152 | tf_op jit(solution)/shard_map/all_to_all | solution.py:283
  130.9 55.5 %copy-start.4 = (f32[16,256]{1,0:T(8,128)}, f32[16,256]{1,0:T(8,128)S(1)}, u32[]{:S(2)}) copy-start(f32[16,256]{1,0:T(8,128)S(1)} %dynamic-slice_add_fusion) | copy-start | bytes 49156
  152.7 5.6 %collective-permute-start.1 = (f32[64,16,256]{2,1,0:T(8,128)S(1)}, f32[64,16,256]{2,1,0:T(8,128)S(1)}, u32[]{:S(2)}, u32[]{:S(2)}) collective-permute-start(f32[64,16,256]{2,1,0:T(8,128)S(1)} %all_to_all.15), channel_id=1, source_target_pairs={{0,1},{1,0},{2,3},{3,2},{4,5},{5,4},{6,7},{7,6},{8,9},{9,8},{10,11... | collective-permute-start | bytes 3145736 | tf_op jit(solution)/shard_map/ppermute | solution.py:288

commit v2 on v1

--- a/solution.py
+++ b/solution.py
@@ -7,6 +7,7 @@
 
 HIGH = lax.Precision.HIGHEST
 F32 = jnp.float32
+OUTER = 32
 
 
 def dot_lead(left, right):
@@ -98,40 +99,98 @@
             work[after:n, :] = rest - change[after - first_lane:, :]
 
 
+def split3(value):
+    high = value.astype(jnp.bfloat16)
+    rest = value - high.astype(F32)
+    middle = rest.astype(jnp.bfloat16)
+    low = (rest - middle.astype(F32)).astype(jnp.bfloat16)
+    return high, middle, low
+
+
+def dot_bf16(left, right, dims):
+    return lax.dot_general(left, right, (dims, ((), ())), preferred_element_type=F32)
+
+
+def gram_of(parts):
+    high, middle, low = parts
+    lead = ((0,), (0,))
+    cross = dot_bf16(high, middle, lead) + dot_bf16(high, low, lead)
+    return dot_bf16(middle, middle, lead) + (cross + cross.T) + dot_bf16(high, high, lead)
+
+
+def times_transposed(parts, right):
+    high, middle, low = parts
+    r_high, r_middle, r_low = split3(right)
+    left = jnp.concatenate([low, middle, high, middle, high, high], axis=1)
+    other = jnp.concatenate([r_high, r_middle, r_low, r_high, r_middle, r_high], axis=1)
+    return dot_bf16(left, other, ((1,), (1,)))
+
+
+def dot_three(left, right, dims):
+    l_high, l_middle, _ = split3(left)
+    r_high, r_middle, _ = split3(right)
+    small = dot_bf16(l_high, r_middle, dims) + dot_bf16(l_middle, r_high, dims)
+    return small + dot_bf16(l_high, r_high, dims)
+
+
+NEAR = 0.0025
+
+
 def tail_kernel(where_ref, mine_ref, other_ref, basis_ref, factor_ref, gram_ref, held, work, upper, first_upper):
     n = work.shape[0]
     rows = basis_ref.shape[0]
     part = mine_ref.shape[0]
     total = float(2 * part)
+    scale = total ** 0.5
     lane = where_ref[0]
     held[pl.ds(pl.multiple_of(lane * part, part), part), :] = mine_ref[...]
     held[pl.ds(pl.multiple_of((1 - lane) * part, part), part), :] = other_ref[...]
     row = lax.broadcasted_iota(jnp.int32, (n, n), 0)
     col = lax.broadcasted_iota(jnp.int32, (n, n), 1)
-    gram1 = dot_lead(held[...], held[...])
+    identity = jnp.where(row == col, 1.0, 0.0)
+    at = pl.multiple_of(where_ref[1], 16)
+    gram1 = gram_of(split3(held[...]))
     gram_ref[...] = gram1 / total
     work[...] = gram1
 
-    def one_pass(step, _):
-        factor_inverse(work, upper, 64)
+    def one_pass(state):
+        step, _ = state
+        factor_inverse(work, upper, OUTER)
+
+        def after_first():
+            first_upper[...] = upper[...]
+            inverse = jnp.where(col <= row, work[...], 0.0)
+            first = times_transposed(split3(held[...]), inverse)
+            held[...] = first
+            gram2 = gram_of(split3(first))
+            work[...] = gram2
+            error = gram2 - identity
+            return jnp.where(jnp.sum(error * error) <= NEAR, 0, 1)
+
+        again = lax.cond(step == 0, after_first, lambda: 0)
+        return step + 1, again
+
+    passes, _ = lax.while_loop(lambda state: state[1] > 0, one_pass, (0, 1))
+
+    @pl.when(passes == 1)
+    def _():
+        error = work[...] - identity
+        weight = jnp.where(col < row, 1.0, jnp.where(col == row, 0.5, 0.0))
+        extra = error * weight
+        for _ in range(2):
+            extra = (error - dot_three(extra, extra, ((1,), (1,)))) * weight
+        square = dot_three(extra, extra, ((1,), (0,)))
+        value = held[pl.ds(at, rows), :]
+        value = value - dot_last(value, extra)
+        value = value + dot_last(value, square)
+        basis_ref[...] = value * scale
+        factor_ref[...] = (first_upper[...] + dot_lead(extra, first_upper[...])) / scale
+
+    @pl.when(passes != 1)
+    def _():
         inverse = jnp.where(col <= row, work[...], 0.0)
-
-        @pl.when(step == 0)
-        def _():
-            first_upper[...] = upper[...]
-            first = dot_last(held[...], inverse)
-            held[...] = first
-            work[...] = dot_lead(first, first)
-
-        @pl.when(step == 1)
-        def _():
-            at = pl.multiple_of(where_ref[1], 16)
-            basis_ref[...] = dot_last(held[pl.ds(at, rows), :], inverse) * (total ** 0.5)
-            factor_ref[...] = jnp.dot(upper[...], first_upper[...], precision=HIGH, preferred_element_type=F32) / (total ** 0.5)
-
-        return 0
-
-    lax.fori_loop(0, 2, one_pass, 0)
+        basis_ref[...] = dot_last(held[pl.ds(at, rows), :], inverse) * scale
+        factor_ref[...] = jnp.dot(upper[...], first_upper[...], precision=HIGH, preferred_element_type=F32) / scale
 
 
 def tail(mine, other, where, rows):
@@ -152,123 +211,193 @@
             pltpu.VMEM((n, n), F32),
             pltpu.VMEM((n, n), F32),
         ],
-        compiler_params=pltpu.CompilerParams(vmem_limit_bytes=48 * 1024 * 1024),
+        compiler_params=pltpu.CompilerParams(vmem_limit_bytes=24 * 1024 * 1024),
     )(where, mine, other)
 
 
-def first_kernel(picks_row, picks_col, energy_row, test, left_x, left_y, packed, diagonal, chosen):
+SIDE = 4
+STRIDE = {"x": 16, "z": 4, "y": 1}
+ORDERS = ("xz", "yx", "zy")
+SWAP = [(0, 1), (1, 0)]
+STEPS = 4
+
+
+def whole(*shape):
+    return pl.BlockSpec(shape, lambda *_: (0,) * len(shape))
+
+
+def image_kernel(half, test, x_long, x_short, y_long, y_short, first, second, third):
+    short = third.shape[1] // 2
+
+    def image(left, weight, out):
+        value = jnp.dot(left[...], test[...], preferred_element_type=F32) * weight
+        return value.reshape(out.shape[0], -1, out.shape[2])
+
+    first[...] = image(x_long, 2.0, first)
+    second[...] = image(y_long, -1.0, second)
+    third[:, :short] = image(x_short, 2.0, third)
+    third[:, short:] = image(y_short, -1.0, third)
+
+
+def image_call(half, exchange, direct, test, room):
+    depth, width = exchange.shape
+    rank = test.shape[1]
+    slices = SIDE * SIDE
+    long, short = 3 * depth // (4 * slices), depth // (4 * slices)
+    per = slices // 2 // STEPS
+    skip = slices * long // (per * short)
+    first_block = pl.BlockSpec((per * long, width), lambda i, half: (half[0] * STEPS + i, 0))
+    second_block = pl.BlockSpec((per * long, width), lambda i, half: (half[1] * STEPS + i, 0))
+    third_block = pl.BlockSpec((per * short, width), lambda i, half: (skip + half[2] * STEPS + i, 0))
+    sizes = [long, long, 2 * short]
+    return pl.pallas_call(
+        image_kernel,
+        grid_spec=pltpu.PrefetchScalarGridSpec(
+            num_scalar_prefetch=1,
+            grid=(STEPS,),
+            in_specs=[whole(width, rank), first_block, third_block, second_block, third_block],
+            out_specs=[pl.BlockSpec((per, size, rank), lambda i, half: (i, 0, 0)) for size in sizes],
+        ),
+        out_shape=[jax.ShapeDtypeStruct((slices // 2, size, rank), F32) for size in sizes],
+        compiler_params=pltpu.CompilerParams(vmem_limit_bytes=room),
+    )(half, test, exchange, exchange, direct, direct)
+
+
+def rows_kernel(picks_row, picks_col, energy_row, test, x_long, x_short, y_long, y_short, packed, diagonal, chosen, held):
     width = test.shape[0]
-    block = left_x.shape[0]
-    cells = packed.shape[0]
-    part = block // cells
     count = picks_col.shape[0]
-
-    @pl.when(pl.program_id(0) == 0)
+    long, short = x_long.shape[0] // SIDE, x_short.shape[0] // SIDE
+    step = pl.program_id(0)
+
+    @pl.when(step == 0)
     def _():
         spot = lax.broadcasted_iota(jnp.int32, (width, 128), 0) == picks_row[...]
         chosen[...] = jnp.where(spot, 1.0, 0.0).astype(jnp.bfloat16)
         here = lax.broadcasted_iota(jnp.int32, (count, width), 1) == picks_col[...]
         energy = jnp.sum(jnp.where(here, energy_row[...], 0.0), axis=1, keepdims=True)
-        taken = lax.dot_general(
-            here.astype(F32).astype(jnp.bfloat16), test[...], (((1,), (0,)), ((), ())), preferred_element_type=F32
-        )
+        taken = jnp.dot(here.astype(F32).astype(jnp.bfloat16), test[...], preferred_element_type=F32)
         diagonal[...] = energy * taken
 
-    right = test[...]
-    own = []
-    for at, (left, weight) in enumerate(((left_x, 2.0), (left_y, -1.0))):
-        image = jnp.dot(left[...], right, preferred_element_type=F32) * weight
-        packed[:, at * part:(at + 1) * part, :] = image.reshape(cells, part, image.shape[1])
-        own.append(jnp.dot(left[...], chosen[...], preferred_element_type=F32).T)
-    for cell in range(cells):
-        pieces = []
-        for group in range(count // 8):
-            for rows in own:
-                pieces.append(rows[8 * group:8 * group + 8, cell * part:(cell + 1) * part])
-        packed[cell, 2 * part:2 * part + 8, :] = jnp.concatenate(pieces, axis=1)
-
-
-def first_call(exchange, direct, test, energies, picks, cells):
+    def own(left):
+        return jnp.dot(left[...], chosen[...], preferred_element_type=F32).T[:count]
+
+    first, second, x_third, y_third = own(x_long), own(y_long), own(x_short), own(y_short)
+    blank = lambda size: jnp.zeros((count, size), F32)
+    for low in range(SIDE):
+        at = step * SIDE + low
+        long_cut, short_cut = slice(low * long, (low + 1) * long), slice(low * short, (low + 1) * short)
+        held[0, at] = jnp.concatenate([first[:, long_cut], blank(long + 2 * short)], axis=1)
+        held[1, at] = jnp.concatenate([blank(long), second[:, long_cut], blank(2 * short)], axis=1)
+        held[2, at] = jnp.concatenate([blank(2 * long), x_third[:, short_cut], y_third[:, short_cut]], axis=1)
+
+    @pl.when(step == SIDE - 1)
+    def _():
+        for x in range(SIDE):
+            for z in range(SIDE):
+                for y in range(SIDE):
+                    cell = x * STRIDE["x"] + z * STRIDE["z"] + y * STRIDE["y"]
+                    value = held[0, x * SIDE + z] + held[1, y * SIDE + x] + held[2, z * SIDE + y]
+                    packed[cell] = value.astype(jnp.bfloat16)
+
+
+def rows_call(exchange, direct, test, energies, picks):
     depth, width = exchange.shape
     rank = test.shape[1]
     count = picks.shape[1]
-    part = depth // cells
-    block = 256
-    per = block // part
+    cells = SIDE ** 3
+    slices = SIDE * SIDE
+    long, short = 3 * depth // (4 * slices), depth // (4 * slices)
+    together = 2 * (long + short)
     picks_row = jnp.pad(picks, ((0, 0), (0, 128 - count)), constant_values=-1)
-    whole = lambda *shape: pl.BlockSpec(shape, lambda i: (0,) * len(shape))
+    long_block = pl.BlockSpec((SIDE * long, width), lambda i: (i, 0))
+    short_block = pl.BlockSpec((SIDE * short, width), lambda i: (3 * SIDE + i, 0))
     return pl.pallas_call(
-        first_kernel,
-        grid=(depth // block,),
+        rows_kernel,
+        grid=(SIDE,),
         in_specs=[
-            whole(1, 128),
-            whole(count, 1),
-            whole(1, width),
-            whole(width, rank),
-            pl.BlockSpec((block, width), lambda i: (i, 0)),
-            pl.BlockSpec((block, width), lambda i: (i, 0)),
+            whole(1, 128), whole(count, 1), whole(1, width), whole(width, rank),
+            long_block, short_block, long_block, short_block,
         ],
-        out_specs=(
-            pl.BlockSpec((per, 2 * part + 8, rank), lambda i: (i, 0, 0)),
-            whole(count, rank),
-        ),
-        out_shape=(
-            jax.ShapeDtypeStruct((cells, 2 * part + 8, rank), F32),
+        out_specs=[whole(cells, count, together), whole(count, rank)],
+        out_shape=[
+            jax.ShapeDtypeStruct((cells, count, together), jnp.bfloat16),
             jax.ShapeDtypeStruct((count, rank), F32),
-        ),
-        scratch_shapes=[pltpu.VMEM((width, 128), jnp.bfloat16)],
-        compiler_params=pltpu.CompilerParams(vmem_limit_bytes=32 * 1024 * 1024),
-    )(picks_row, picks.reshape(count, 1), energies.reshape(1, width), test, exchange, direct)
-
-
-def split3(value):
-    high = value.astype(jnp.bfloat16)
-    rest = value - high.astype(F32)
-    middle = rest.astype(jnp.bfloat16)
-    low = (rest - middle.astype(F32)).astype(jnp.bfloat16)
-    return high, middle, low
-
-
-def couple_kernel(lane_ref, packed, keep, give):
-    cells, height, rank = packed.shape
-    depth = height - 8
-    image = packed[0, :depth, :]
-    for cell in range(1, cells):
-        image = image + packed[cell, :depth, :]
+        ],
+        scratch_shapes=[
+            pltpu.VMEM((width, 128), jnp.bfloat16),
+            pltpu.VMEM((3, slices, count, together), F32),
+        ],
+        compiler_params=pltpu.CompilerParams(vmem_limit_bytes=56 * 1024 * 1024),
+    )(picks_row, picks.reshape(count, 1), energies.reshape(1, width), test, exchange, exchange, direct, direct)
+
+
+def merge_kernel(bits, *refs):
+    kept, came, give, keep = refs[0:3], refs[3:6], refs[6:9], refs[9:12]
+    for part in range(3):
+        size = give[part].shape[0]
+        bit = bits[part]
+        away, stay = pl.ds((1 - bit) * size, size), pl.ds(bit * size, size)
+        give[part][...] = kept[part][away] + came[part][away]
+        keep[part][...] = kept[part][stay] + came[part][stay]
+
+
+def merge(bits, kept, came):
+    vmem = pl.BlockSpec(memory_space=pltpu.VMEM)
+    shapes = [jax.ShapeDtypeStruct((k.shape[0] // 2,) + k.shape[1:], F32) for k in kept]
+    made = pl.pallas_call(
+        merge_kernel,
+        out_shape=shapes + shapes,
+        in_specs=[pl.BlockSpec(memory_space=pltpu.SMEM)] + [vmem] * 6,
+        out_specs=[vmem] * 6,
+        compiler_params=pltpu.CompilerParams(vmem_limit_bytes=16 * 1024 * 1024),
+    )(bits, *kept, *came)
+    return list(made[:3]), list(made[3:])
+
+
+def couple_kernel(lane_ref, first, second, third, packed, keep, give):
+    cells, count, together = packed.shape
+    rank = first.shape[-1]
+    half_rows = count // 2
+    image = jnp.concatenate([first[0], second[0], third[0]], axis=0)
     parts = split3(image)
-    rows = packed[:, depth:, :].reshape(cells * 8, rank).astype(jnp.bfloat16)
     lane = lane_ref[0]
-    for group in range(rank // depth):
-        left = rows[:, group * depth:(group + 1) * depth]
-        out = jnp.zeros((cells * 8, rank), F32)
+    for half in range(2):
+        left = packed[:, half * half_rows:(half + 1) * half_rows, :].reshape(cells * half_rows, together)
+        out = jnp.zeros((cells * half_rows, rank), F32)
         for piece in reversed(parts):
             out = out + jnp.dot(left, piece, preferred_element_type=F32)
-        out = out.reshape(cells, 8, rank)
-        half, at = group // 2, group % 2 * 8
+        out = out.reshape(cells, half_rows, rank)
 
         @pl.when(lane == half)
         def _():
-            keep[:, at:at + 8, :] = out
+            keep[...] = out
 
         @pl.when(lane != half)
         def _():
-            give[:, at:at + 8, :] = out
-
-
-def couple(lane, packed):
-    cells, height, rank = packed.shape
+            give[...] = out
+
+
+def couple(lane, parts, packed):
+    cells, count, _ = packed.shape
+    rank = parts[0].shape[-1]
     vmem = pl.BlockSpec(memory_space=pltpu.VMEM)
-    shape = jax.ShapeDtypeStruct((cells, 16, rank), F32)
+    shape = jax.ShapeDtypeStruct((cells, count // 2, rank), F32)
     return pl.pallas_call(
         couple_kernel,
         out_shape=(shape, shape),
-        in_specs=[pl.BlockSpec(memory_space=pltpu.SMEM), vmem],
+        in_specs=[pl.BlockSpec(memory_space=pltpu.SMEM)] + [vmem] * 4,
         out_specs=(vmem, vmem),
-        compiler_params=pltpu.CompilerParams(vmem_limit_bytes=40 * 1024 * 1024),
-    )(lane, packed)
-
-
-SWAP = [(0, 1), (1, 0)]
+        compiler_params=pltpu.CompilerParams(vmem_limit_bytes=16 * 1024 * 1024),
+    )(lane, *parts, packed)
+
+
+def neighbours(axis, far):
+    pairs = []
+    for device in range(SIDE ** 3):
+        at = device // STRIDE[axis] % SIDE
+        to = SIDE - 1 - at if far else at ^ 1
+        pairs.append((device, device + (to - at) * STRIDE[axis]))
+    return pairs
 
 
 def shards(exchange_pairs, direct_pairs, test_matrix, energies, picks):
@@ -276,17 +405,44 @@
     lane = lax.axis_index("pw")
     place = lax.axis_index("col")
     lane_ref = lane.astype(jnp.int32).reshape(1)
-    packed, diagonal = first_call(exchange_pairs, direct_pairs, test_matrix, energies, picks, cells)
+    at = {axis: place // STRIDE[axis] % SIDE for axis in "xyz"}
+    far = jnp.stack([at[order[0]] // 2 for order in ORDERS]).astype(jnp.int32)
+    near = jnp.stack([at[order[0]] % 2 for order in ORDERS]).astype(jnp.int32)
+    gives = image_call(1 - far, exchange_pairs, direct_pairs, test_matrix, 56 * 1024 * 1024)
+    picks, gives = lax.optimization_barrier((picks, gives))
+    came = [lax.ppermute(give, "col", neighbours(order[0], True)) for give, order in zip(gives, ORDERS)]
+    packed, diagonal = rows_call(exchange_pairs, direct_pairs, test_matrix, energies, picks)
+    far, packed, diagonal = lax.optimization_barrier((far, packed, diagonal))
+    keeps = image_call(far, exchange_pairs, direct_pairs, test_matrix, 56 * 1024 * 1024)
     packed = lax.all_to_all(packed, "col", split_axis=0, concat_axis=0, tiled=True)
-    keep, give = couple(lane_ref, packed)
+    gives, keeps = merge(near, keeps, came)
+    for step in range(1, 4):
+        if step > 1:
+            for part, order in enumerate(ORDERS):
+                size = keeps[part].shape[0] // 2
+                coordinate = at[order[1]]
+                bit = coordinate // 2 if step == 2 else coordinate % 2
+                value = keeps[part]
+                gives[part] = lax.dynamic_slice_in_dim(value, (1 - bit) * size, size, 0)
+                keeps[part] = lax.dynamic_slice_in_dim(value, bit * size, size, 0)
+        if step == 2:
+            gives, packed, diagonal = lax.optimization_barrier((gives, packed, diagonal))
+        else:
+            gives = lax.optimization_barrier(gives)
+        gives = list(gives)
+        for part, order in enumerate(ORDERS):
+            keeps[part] = keeps[part] + lax.ppermute(gives[part], "col", neighbours(order[step // 2], step % 2 == 0))
+    keep, give = couple(lane_ref, keeps, packed)
     both = keep + lax.ppermute(give, "pw", SWAP)
+    half = both.shape[1]
+    own_diagonal = lax.dynamic_slice_in_dim(diagonal, lane * half, half, 0)
+    where = jnp.stack([lane, lane * (cells * half) + place * half]).astype(jnp.int32)
+    both, own_diagonal, where = lax.optimization_barrier((both, own_diagonal, where))
     arrived = lax.all_to_all(both, "col", split_axis=0, concat_axis=0, tiled=True)
-    half = both.shape[1]
-    sketch = jnp.sum(arrived, axis=0) + lax.dynamic_slice_in_dim(diagonal, lane * half, half, 0)
+    sketch = jnp.sum(arrived, axis=0) + own_diagonal
     copies = jnp.broadcast_to(sketch[None], (cells,) + sketch.shape)
     mine = lax.all_to_all(copies, "col", split_axis=0, concat_axis=0, tiled=True)
     other = lax.ppermute(mine, "pw", SWAP)
-    where = jnp.stack([lane, lane * (cells * half) + place * half]).astype(jnp.int32)
     rank = sketch.shape[1]
     basis, factor, gram = tail(mine.reshape(cells * half, rank), other.reshape(cells * half, rank), where, half)
     return (sketch, basis, factor, gram)

time: 187 us -> 151 us (0.81)
  waiting for transfers between devices: 79.1 us -> 16 us
  blocking collectives: 21.6 us -> 46 us
  other arithmetic: 1.36 us -> 4.47 us
  Pallas kernels: 39.8 us -> 41.8 us
  local copies, waits for them, and re-layouts: 9.48 us -> 7.48 us
    all_to_all x1, waiting for transfers between devices: 57.6 us -> 0.01 us  [shards(): lax.all_to_all(packed, 'col', split_axis=0, concat_axis=0, tiled=True)]
    all_to_all x0 -> x1, blocking collectives: none -> 24.4 us  [shards(): lax.all_to_all(both, 'col', split_axis=0, concat_axis=0, tiled=True)]
    ppermute x0 -> x12, starting transfers between devices: none -> 20.2 us  [the longest x9 10.4 us: shards(): lax.ppermute(gives[part], 'col', neighbours(order[step // 2], step % 2 ==...]
    all_to_all x1 -> x0, waiting for transfers between devices: 17 us -> none  [shards(): lax.all_to_all(both, 'col', split_axis=0, concat_axis=0, tiled=True)]
    all_to_all x1 -> x0, starting transfers between devices: 14.9 us -> none  [shards(): lax.all_to_all(both, 'col', split_axis=0, concat_axis=0, tiled=True)]
    pallas_call x1 -> x4, Pallas kernels: 6.77 us -> 20.7 us  [the longest x2 11.6 us: image_call(): pl.pallas_call(image_kernel, grid_spec=pltpu.PrefetchScalarGridSpec(num_s...]
    ppermute x0 -> x12, waiting for transfers between devices: none -> 12.1 us  [the longest x9 12.1 us: shards(): lax.ppermute(gives[part], 'col', neighbours(order[step // 2], step % 2 ==...]
    pallas_call x1, Pallas kernels: 28.1 us -> 19.1 us  [tail(): pl.pallas_call(tail_kernel, out_shape=(jax.ShapeDtypeStruct((rows, n), F3...]
  transfers between devices with their start and end apart: 4 -> 15, of which waited for: 4 -> 9; matrix products, arithmetic and copies ran while one was open for 0% -> 3% of each run, Pallas kernels for 0% -> 10%
where the time goes in v2:
time: 151 us
  blocking collectives  46 us (30%)
  Pallas kernels  41.8 us (28%)
  starting transfers between devices  33.8 us (22%)
  waiting for transfers between devices  16 us (11%)
  local copies, waits for them, and re-layouts  7.48 us (5%)
  other arithmetic  4.47 us (3%)
    all_to_all x1, blocking collectives, shards(): lax.all_to_all(both, 'col', split_axis=0, concat_axis=0, tiled=True)  24.4 us
    all_to_all x1, blocking collectives, shards(): lax.all_to_all(copies, 'col', split_axis=0, concat_axis=0, tiled=True)  21.6 us
    pallas_call x1, Pallas kernels, tail(): pl.pallas_call(tail_kernel, out_shape=(jax.ShapeDtypeStruct((rows, n), F3...  19.1 us
    ppermute x9, waiting for transfers between devices, shards(): lax.ppermute(gives[part], 'col', neighbours(order[step // 2], step % 2 ==...  12.1 us
    pallas_call x2, Pallas kernels, image_call(): pl.pallas_call(image_kernel, grid_spec=pltpu.PrefetchScalarGridSpec(num_s...  11.6 us
    ppermute x9, starting transfers between devices, shards(): lax.ppermute(gives[part], 'col', neighbours(order[step // 2], step % 2 ==...  10.4 us
    ppermute x3, starting transfers between devices, shards(): lax.ppermute(give, 'col', neighbours(order[0], True))  9.8 us
    pallas_call x1, Pallas kernels, rows_call(): pl.pallas_call(rows_kernel, grid=(SIDE,), in_specs=[whole(1, 128), whole(...  7.47 us
  transfers between devices with their start and end apart: 15, of which 9 were waited for; matrix products, arithmetic and copies ran while one was open for 3% of the time, Pallas kernels for 10%

profile of v2, /device:TPU:1, one launch (start us, length us, event | category | flops | bytes accessed | tf_op | source)
XLA Modules:
  0.0 150.6 jit_solution(13884283236033725355)
XLA Ops:
  0.8 0.6 broadcast_subtract_fusion
  1.4 0.0 copy-start.7
  1.4 0.0 copy-start.6
  1.4 5.8 %shard_map.84 = (f32[8,96,256]{2,1,0:T(8,128)}, f32[8,96,256]{2,1,0:T(8,128)}, f32[8,64,256]{2,1,0:T(8,128)}) custom-call(s32[3]{0:T(128)} %get-tuple-element.84.half, bf16[896,256]{1,0:T(8,128)(2,1)} %test.5, bf16[2048,896]{1,0:T(8,128)(2,1)} %x_short.5, bf16[2048,896]{1,0:T(8,128)(2,1)} %x_short.5, bf16[2048,896]{1,0:T(8,128)(2,1)} %y_short.5, ...), custom_call_target="tpu_custom_call" | custom-call | tf_op jit(solution)/shard_map/pallas_call | solution.py:253
  7.2 3.3 %collective-permute-start = (f32[8,96,256]{2,1,0:T(8,128)}, f32[8,96,256]{2,1,0:T(8,128)S(1)}, u32[]{:S(2)}, u32[]{:S(2)}) collective-permute-start(f32[8,96,256]{2,1,0:T(8,128)} %get-tuple-element.54), channel_id=1, source_target_pairs={{0,96},{2,98},{4,100},{6,102},{8,104},{10,106},{12,108},{14,110},{... | collective-permute-start | bytes 2359304 | tf_op jit(solution)/shard_map/ppermute | solution.py:413
  10.5 2.7 %collective-permute-start.1 = (f32[8,96,256]{2,1,0:T(8,128)}, f32[8,96,256]{2,1,0:T(8,128)S(1)}, u32[]{:S(2)}, u32[]{:S(2)}) collective-permute-start(f32[8,96,256]{2,1,0:T(8,128)} %get-tuple-element.55), channel_id=1, source_target_pairs={{0,6},{2,4},{4,2},{6,0},{8,14},{10,12},{12,10},{14,8},{16,22},{18,... | collective-permute-start | bytes 2359304 | tf_op jit(solution)/shard_map/ppermute | solution.py:413
  13.2 3.8 %collective-permute-start.2 = (f32[8,64,256]{2,1,0:T(8,128)}, f32[8,64,256]{2,1,0:T(8,128)S(1)}, u32[]{:S(2)}, u32[]{:S(2)}) collective-permute-start(f32[8,64,256]{2,1,0:T(8,128)} %get-tuple-element.56), channel_id=1, source_target_pairs={{0,24},{2,26},{4,28},{6,30},{8,16},{10,18},{12,20},{14,22},{16,8},... | collective-permute-start | bytes 1572872 | tf_op jit(solution)/shard_map/ppermute | solution.py:413
  17.0 0.0 copy-done.7
  17.0 0.5 pad.4.picks_row
  17.5 0.7 copy.9.picks_col
  18.2 0.0 copy-done.6
  18.2 0.6 reshape.26.energy_row
  18.8 7.5 %shard_map.85 = (bf16[64,32,256]{2,1,0:T(8,128)(2,1)}, f32[32,256]{1,0:T(8,128)}) custom-call(s32[1,128]{1,0:T(1,128)} %pad.4.picks_row, s32[32,1]{1,0:T(8,128)} %copy.9.picks_col, f32[1,896]{1,0:T(1,128)} %reshape.26.energy_row, bf16[896,256]{1,0:T(8,128)(2,1)} %test.5, bf16[2048,896]{1,0:T(8,128)(2,1)} %x_short.5, bf16[2048,896]{1,0:T(8,128)(2,1)} %x_short.5, ...), custom_call_target="tpu_custom_call" | custom-call | tf_op jit(solution)/shard_map/pallas_call | solution.py:314
  26.2 4.7 %all-to-all-start = ((bf16[64,32,256]{2,1,0:T(8,128)(2,1)}), bf16[64,32,256]{2,1,0:T(8,128)(2,1)S(1)}, u32[]{:S(2)}, u32[]{:S(2)}) async-start(bf16[64,32,256]{2,1,0:T(8,128)(2,1)} %get-tuple-element.66), calls=%async_computation | async-start | bytes 2097152 | tf_op jit(solution)/shard_map/all_to_all | solution.py:417
  30.9 5.8 %shard_map.86 = (f32[8,96,256]{2,1,0:T(8,128)}, f32[8,96,256]{2,1,0:T(8,128)}, f32[8,64,256]{2,1,0:T(8,128)}) custom-call(s32[3]{0:T(128)} %get-tuple-element.50.half, bf16[896,256]{1,0:T(8,128)(2,1)} %test.5, bf16[2048,896]{1,0:T(8,128)(2,1)} %x_short.5, bf16[2048,896]{1,0:T(8,128)(2,1)} %x_short.5, bf16[2048,896]{1,0:T(8,128)(2,1)} %y_short.5, ...), custom_call_target="tpu_custom_call" | custom-call | tf_op jit(solution)/shard_map/pallas_call | solution.py:253
  36.7 0.1 pad_add_fusion.bits
  36.8 0.0 collective-permute-done.2.refs_5_
  36.8 0.0 collective-permute-done.refs_3_
  36.8 0.0 collective-permute-done.1.refs_4_
  36.8 0.0 copy-start
  36.8 1.1 copy-done
  37.9 0.0 copy-start.1
  37.9 1.1 copy-done.1
  39.0 1.0 copy-done.2
  40.1 1.6 %shard_map.87 = (f32[4,96,256]{2,1,0:T(8,128)}, f32[4,96,256]{2,1,0:T(8,128)}, f32[4,64,256]{2,1,0:T(8,128)}, f32[4,96,256]{2,1,0:T(8,128)S(1)}, f32[4,96,256]{2,1,0:T(8,128)S(1)}, /*index=5*/f32[4,64,256]{2,1,0:T(8,128)S(1)}) custom-call(s32[3]{0:T(128)S(1)} %pad_add_fusion.bits, f32[8,96,256]{2,1,0:T(8,128)S(1)} %copy-done, f32[8,96,256]{2,1,0:T(8,128)S(1)} %copy-done.1, ...), custom_call_target="tpu_custom_call" | custom-call | tf_op jit(solution)/shard_map/pallas_call | solution.py:347
  41.7 0.7 copy-done.3
  42.4 0.7 copy-done.4
  43.1 0.9 collective-permute-start.4
  44.0 1.3 collective-permute-start.3
  45.3 1.2 collective-permute-start.5
  46.5 4.5 %collective-permute-done.5 = f32[4,64,256]{2,1,0:T(8,128)S(1)} collective-permute-done((f32[4,64,256]{2,1,0:T(8,128)}, f32[4,64,256]{2,1,0:T(8,128)S(1)}, u32[]{:S(2)}, u32[]{:S(2)}) %collective-permute-start.5) | collective-permute-done | bytes 262176 | tf_op jit(solution)/shard_map/ppermute | solution.py:434
  51.0 1.0 add.119
  52.1 0.7 collective-permute-done.4
  52.8 1.0 add.117
  53.8 0.0 collective-permute-done.3
  53.8 0.1 add.114
  54.0 0.0 all-to-all-done.packed
  54.0 1.6 %collective-permute-start.8 = (f32[2,64,256]{2,1,0:T(8,128)S(1)}, f32[2,64,256]{2,1,0:T(8,128)S(1)}, u32[]{:S(2)}, u32[]{:S(2)}) collective-permute-start(f32[2,64,256]{2,1,0:T(8,128)S(1)} %constant_dynamic-slice_fusion.4), channel_id=1, source_target_pairs={{0,6},{2,4},{4,2},{6,0},{8,14},{10,12},{12,10},{14,8},{16,22},{18,... | collective-permute-start | bytes 393224 | tf_op jit(solution)/shard_map/ppermute | solution.py:434
  55.5 2.7 %collective-permute-start.7 = (f32[2,96,256]{2,1,0:T(8,128)S(1)}, f32[2,96,256]{2,1,0:T(8,128)S(1)}, u32[]{:S(2)}, u32[]{:S(2)}) collective-permute-start(f32[2,96,256]{2,1,0:T(8,128)S(1)} %constant_dynamic-slice_fusion.5), channel_id=1, source_target_pairs={{0,96},{2,98},{4,100},{6,102},{8,104},{10,106},{12,108},{14,110},{... | collective-permute-start | bytes 589832 | tf_op jit(solution)/shard_map/ppermute | solution.py:434
  58.3 2.5 %collective-permute-start.6 = (f32[2,96,256]{2,1,0:T(8,128)S(1)}, f32[2,96,256]{2,1,0:T(8,128)S(1)}, u32[]{:S(2)}, u32[]{:S(2)}) collective-permute-start(f32[2,96,256]{2,1,0:T(8,128)S(1)} %constant_dynamic-slice_fusion.6), channel_id=1, source_target_pairs={{0,24},{2,26},{4,28},{6,30},{8,16},{10,18},{12,20},{14,22},{16,8},... | collective-permute-start | bytes 589832 | tf_op jit(solution)/shard_map/ppermute | solution.py:434
  60.7 0.0 collective-permute-done.8
  60.8 0.8 collective-permute-done.7
  61.7 2.6 %collective-permute-done.6 = f32[2,96,256]{2,1,0:T(8,128)S(1)} collective-permute-done((f32[2,96,256]{2,1,0:T(8,128)S(1)}, f32[2,96,256]{2,1,0:T(8,128)S(1)}, u32[]{:S(2)}, u32[]{:S(2)}) %collective-permute-start.6) | collective-permute-done | bytes 196640 | tf_op jit(solution)/shard_map/ppermute | solution.py:434
  64.3 0.1 collective-permute-start.11
  64.5 0.1 collective-permute-start.10
  64.6 0.1 collective-permute-start.9
  64.6 3.2 %collective-permute-done.11 = f32[1,64,256]{2,1,0:T(8,128)S(1)} collective-permute-done((f32[1,64,256]{2,1,0:T(8,128)S(1)}, f32[1,64,256]{2,1,0:T(8,128)S(1)}, u32[]{:S(2)}, u32[]{:S(2)}) %collective-permute-start.11) | collective-permute-done | bytes 65568 | tf_op jit(solution)/shard_map/ppermute | solution.py:434
  67.8 0.2 collective-permute-done.10
  68.0 0.1 collective-permute-done.9
  68.1 2.1 %shard_map.88 = (f32[64,16,256]{2,1,0:T(8,128)S(1)}, f32[64,16,256]{2,1,0:T(8,128)S(1)}) custom-call(s32[1]{0:T(128)} %bitcast.lane_ref, f32[1,96,256]{2,1,0:T(8,128)S(1)} %dynamic-slice_add_fusion.4.first, f32[1,96,256]{2,1,0:T(8,128)S(1)} %dynamic-slice_add_fusion.3.second, f32[1,64,256]{2,1,0:T(8,128)S(1)} %dynamic-slice_add_fusion.5.third, ...), custom_call_target="tpu_custom_call" | custom-call | tf_op jit(solution)/shard_map/pallas_call | solution.py:385
  70.2 5.7 %collective-permute-start.12 = (f32[64,16,256]{2,1,0:T(8,128)S(1)}, f32[64,16,256]{2,1,0:T(8,128)}, u32[]{:S(2)}, u32[]{:S(2)}) collective-permute-start(f32[64,16,256]{2,1,0:T(8,128)S(1)} %get-tuple-element.76), channel_id=1, source_target_pairs={{0,1},{1,0},{2,3},{3,2},{4,5},{5,4},{6,7},{7,6},{8,9},{9,8},{10,11... | collective-permute-start | bytes 3145736 | tf_op jit(solution)/shard_map/ppermute | solution.py:436
  75.9 0.1 pad_add_fusion.2.where_ref
  75.9 0.7 constant_dynamic-slice_fusion
  76.7 1.6 %collective-permute-done.12 = f32[64,16,256]{2,1,0:T(8,128)} collective-permute-done((f32[64,16,256]{2,1,0:T(8,128)S(1)}, f32[64,16,256]{2,1,0:T(8,128)}, u32[]{:S(2)}, u32[]{:S(2)}) %collective-permute-start.12) | collective-permute-done | bytes 1048608 | tf_op jit(solution)/shard_map/ppermute | solution.py:436
  78.3 1.4 add.135
  79.7 24.4 %all_to_all.15 = f32[64,16,256]{2,1,0:T(8,128)S(1)} all-to-all(f32[64,16,256]{2,1,0:T(8,128)S(1)} %add.135), channel_id=1, replica_groups=mesh['col'=64,'pw'=2] {'col'}, dimensions={0} | all-to-all | bytes 2097152 | tf_op jit(solution)/shard_map/all_to_all | solution.py:441
  104.1 0.1 reduce_sum.9
  104.2 0.0 copy-start.5
  104.2 0.1 broadcast_in_dim.2
  104.3 21.6 %all_to_all.16 = f32[64,16,256]{2,1,0:T(8,128)S(1)} all-to-all(f32[64,16,256]{2,1,0:T(8,128)S(1)} %broadcast_in_dim.2), channel_id=1, replica_groups=mesh['col'=64,'pw'=2] {'col'}, dimensions={0} | all-to-all | bytes 2097152 | tf_op jit(solution)/shard_map/all_to_all | solution.py:444
  126.0 3.3 %collective-permute-start.13 = (f32[64,16,256]{2,1,0:T(8,128)S(1)}, f32[64,16,256]{2,1,0:T(8,128)S(1)}, u32[]{:S(2)}, u32[]{:S(2)}) collective-permute-start(f32[64,16,256]{2,1,0:T(8,128)S(1)} %all_to_all.16), channel_id=1, source_target_pairs={{0,1},{1,0},{2,3},{3,2},{4,5},{5,4},{6,7},{7,6},{8,9},{9,8},{10,11... | collective-permute-start | bytes 3145736 | tf_op jit(solution)/shard_map/ppermute | solution.py:445
  129.2 2.3 %collective-permute-done.13 = f32[64,16,256]{2,1,0:T(8,128)S(1)} collective-permute-done((f32[64,16,256]{2,1,0:T(8,128)S(1)}, f32[64,16,256]{2,1,0:T(8,128)S(1)}, u32[]{:S(2)}, u32[]{:S(2)}) %collective-permute-start.13) | collective-permute-done | bytes 1048608 | tf_op jit(solution)/shard_map/ppermute | solution.py:445
  131.5 19.1 %shard_map.89 = (f32[16,256]{1,0:T(8,128)}, f32[256,256]{1,0:T(8,128)}, f32[256,256]{1,0:T(8,128)}) custom-call(s32[2]{0:T(128)S(1)} %pad_add_fusion.2.where_ref, f32[1024,256]{1,0:T(8,128)S(1)} %bitcast.11, f32[1024,256]{1,0:T(8,128)S(1)} %bitcast.12), custom_call_target="tpu_custom_call" | custom-call | tf_op jit(solution)/shard_map/pallas_call | solution.py:199
  150.6 0.0 copy-done.5
  (16 shorter events, 0.2 us)
Async XLA Ops:
  1.4 15.6 %copy-start.7 = (s32[1,32]{1,0:T(1,128)S(1)}, s32[1,32]{1,0:T(1,128)}, u32[]{:S(2)}) copy-start(s32[1,32]{1,0:T(1,128)} %param.9) | copy-start | bytes 388
  1.4 16.8 %copy-start.6 = (f32[896]{0:T(1024)S(1)}, f32[896]{0:T(1024)}, u32[]{:S(2)}) copy-start(f32[896]{0:T(1024)} %param.8) | copy-start | bytes 10756
  7.2 29.6 %collective-permute-start = (f32[8,96,256]{2,1,0:T(8,128)}, f32[8,96,256]{2,1,0:T(8,128)S(1)}, u32[]{:S(2)}, u32[]{:S(2)}) collective-permute-start(f32[8,96,256]{2,1,0:T(8,128)} %get-tuple-element.54), channel_id=1, source_target_pairs={{0,96},{2,98},{4,100},{6,102},{8,104},{10,106},{12,108},{14,110},{... | collective-permute-start | bytes 2359304 | tf_op jit(solution)/shard_map/ppermute | solution.py:413
  10.5 26.3 %collective-permute-start.1 = (f32[8,96,256]{2,1,0:T(8,128)}, f32[8,96,256]{2,1,0:T(8,128)S(1)}, u32[]{:S(2)}, u32[]{:S(2)}) collective-permute-start(f32[8,96,256]{2,1,0:T(8,128)} %get-tuple-element.55), channel_id=1, source_target_pairs={{0,6},{2,4},{4,2},{6,0},{8,14},{10,12},{12,10},{14,8},{16,22},{18,... | collective-permute-start | bytes 2359304 | tf_op jit(solution)/shard_map/ppermute | solution.py:413
  13.2 23.5 %collective-permute-start.2 = (f32[8,64,256]{2,1,0:T(8,128)}, f32[8,64,256]{2,1,0:T(8,128)S(1)}, u32[]{:S(2)}, u32[]{:S(2)}) collective-permute-start(f32[8,64,256]{2,1,0:T(8,128)} %get-tuple-element.56), channel_id=1, source_target_pairs={{0,24},{2,26},{4,28},{6,30},{8,16},{10,18},{12,20},{14,22},{16,8},... | collective-permute-start | bytes 1572872 | tf_op jit(solution)/shard_map/ppermute | solution.py:413
  26.2 27.7 %all-to-all-start = ((bf16[64,32,256]{2,1,0:T(8,128)(2,1)}), bf16[64,32,256]{2,1,0:T(8,128)(2,1)S(1)}, u32[]{:S(2)}, u32[]{:S(2)}) async-start(bf16[64,32,256]{2,1,0:T(8,128)(2,1)} %get-tuple-element.66), calls=%async_computation | async-start | bytes 2097152 | tf_op jit(solution)/shard_map/all_to_all | solution.py:417
  36.8 1.1 copy-start
  37.9 1.1 copy-start.1
  39.0 1.0 copy-start.2
  41.7 0.7 copy-start.3
  42.4 0.7 copy-start.4
  43.1 9.7 %collective-permute-start.4 = (f32[4,96,256]{2,1,0:T(8,128)}, f32[4,96,256]{2,1,0:T(8,128)S(1)}, u32[]{:S(2)}, u32[]{:S(2)}) collective-permute-start(f32[4,96,256]{2,1,0:T(8,128)} %get-tuple-element.63), channel_id=1, source_target_pairs={{0,2},{2,0},{4,6},{6,4},{8,10},{10,8},{12,14},{14,12},{16,18},{18,... | collective-permute-start | bytes 1179656 | tf_op jit(solution)/shard_map/ppermute | solution.py:434
  44.0 9.8 %collective-permute-start.3 = (f32[4,96,256]{2,1,0:T(8,128)}, f32[4,96,256]{2,1,0:T(8,128)S(1)}, u32[]{:S(2)}, u32[]{:S(2)}) collective-permute-start(f32[4,96,256]{2,1,0:T(8,128)} %get-tuple-element.61), channel_id=1, source_target_pairs={{0,32},{2,34},{4,36},{6,38},{8,40},{10,42},{12,44},{14,46},{16,48}... | collective-permute-start | bytes 1179656 | tf_op jit(solution)/shard_map/ppermute | solution.py:434
  45.3 5.7 %collective-permute-start.5 = (f32[4,64,256]{2,1,0:T(8,128)}, f32[4,64,256]{2,1,0:T(8,128)S(1)}, u32[]{:S(2)}, u32[]{:S(2)}) collective-permute-start(f32[4,64,256]{2,1,0:T(8,128)} %get-tuple-element.65), channel_id=1, source_target_pairs={{0,8},{2,10},{4,12},{6,14},{8,0},{10,2},{12,4},{14,6},{16,24},{18,... | collective-permute-start | bytes 786440 | tf_op jit(solution)/shard_map/ppermute | solution.py:434
  54.0 6.8 %collective-permute-start.8 = (f32[2,64,256]{2,1,0:T(8,128)S(1)}, f32[2,64,256]{2,1,0:T(8,128)S(1)}, u32[]{:S(2)}, u32[]{:S(2)}) collective-permute-start(f32[2,64,256]{2,1,0:T(8,128)S(1)} %constant_dynamic-slice_fusion.4), channel_id=1, source_target_pairs={{0,6},{2,4},{4,2},{6,0},{8,14},{10,12},{12,10},{14,8},{16,22},{18,... | collective-permute-start | bytes 393224 | tf_op jit(solution)/shard_map/ppermute | solution.py:434
  55.5 6.1 %collective-permute-start.7 = (f32[2,96,256]{2,1,0:T(8,128)S(1)}, f32[2,96,256]{2,1,0:T(8,128)S(1)}, u32[]{:S(2)}, u32[]{:S(2)}) collective-permute-start(f32[2,96,256]{2,1,0:T(8,128)S(1)} %constant_dynamic-slice_fusion.5), channel_id=1, source_target_pairs={{0,96},{2,98},{4,100},{6,102},{8,104},{10,106},{12,108},{14,110},{... | collective-permute-start | bytes 589832 | tf_op jit(solution)/shard_map/ppermute | solution.py:434
  58.3 6.0 %collective-permute-start.6 = (f32[2,96,256]{2,1,0:T(8,128)S(1)}, f32[2,96,256]{2,1,0:T(8,128)S(1)}, u32[]{:S(2)}, u32[]{:S(2)}) collective-permute-start(f32[2,96,256]{2,1,0:T(8,128)S(1)} %constant_dynamic-slice_fusion.6), channel_id=1, source_target_pairs={{0,24},{2,26},{4,28},{6,30},{8,16},{10,18},{12,20},{14,22},{16,8},... | collective-permute-start | bytes 589832 | tf_op jit(solution)/shard_map/ppermute | solution.py:434
  64.3 3.5 %collective-permute-start.11 = (f32[1,64,256]{2,1,0:T(8,128)S(1)}, f32[1,64,256]{2,1,0:T(8,128)S(1)}, u32[]{:S(2)}, u32[]{:S(2)}) collective-permute-start(f32[1,64,256]{2,1,0:T(8,128)S(1)} %constant_dynamic-slice_fusion.1), channel_id=1, source_target_pairs={{0,2},{2,0},{4,6},{6,4},{8,10},{10,8},{12,14},{14,12},{16,18},{18,... | collective-permute-start | bytes 196616 | tf_op jit(solution)/shard_map/ppermute | solution.py:434
  64.5 3.6 %collective-permute-start.10 = (f32[1,96,256]{2,1,0:T(8,128)S(1)}, f32[1,96,256]{2,1,0:T(8,128)S(1)}, u32[]{:S(2)}, u32[]{:S(2)}) collective-permute-start(f32[1,96,256]{2,1,0:T(8,128)S(1)} %constant_dynamic-slice_fusion.2), channel_id=1, source_target_pairs={{0,32},{2,34},{4,36},{6,38},{8,40},{10,42},{12,44},{14,46},{16,48}... | collective-permute-start | bytes 294920 | tf_op jit(solution)/shard_map/ppermute | solution.py:434
  64.6 3.5 %collective-permute-start.9 = (f32[1,96,256]{2,1,0:T(8,128)S(1)}, f32[1,96,256]{2,1,0:T(8,128)S(1)}, u32[]{:S(2)}, u32[]{:S(2)}) collective-permute-start(f32[1,96,256]{2,1,0:T(8,128)S(1)} %constant_dynamic-slice_fusion.3), channel_id=1, source_target_pairs={{0,8},{2,10},{4,12},{6,14},{8,0},{10,2},{12,4},{14,6},{16,24},{18,... | collective-permute-start | bytes 294920 | tf_op jit(solution)/shard_map/ppermute | solution.py:434
  70.2 8.1 %collective-permute-start.12 = (f32[64,16,256]{2,1,0:T(8,128)S(1)}, f32[64,16,256]{2,1,0:T(8,128)}, u32[]{:S(2)}, u32[]{:S(2)}) collective-permute-start(f32[64,16,256]{2,1,0:T(8,128)S(1)} %get-tuple-element.76), channel_id=1, source_target_pairs={{0,1},{1,0},{2,3},{3,2},{4,5},{5,4},{6,7},{7,6},{8,9},{9,8},{10,11... | collective-permute-start | bytes 3145736 | tf_op jit(solution)/shard_map/ppermute | solution.py:436
  104.2 46.4 %copy-start.5 = (f32[16,256]{1,0:T(8,128)}, f32[16,256]{1,0:T(8,128)S(1)}, u32[]{:S(2)}) copy-start(f32[16,256]{1,0:T(8,128)S(1)} %add.138) | copy-start | bytes 49156
  126.0 5.6 %collective-permute-start.13 = (f32[64,16,256]{2,1,0:T(8,128)S(1)}, f32[64,16,256]{2,1,0:T(8,128)S(1)}, u32[]{:S(2)}, u32[]{:S(2)}) collective-permute-start(f32[64,16,256]{2,1,0:T(8,128)S(1)} %all_to_all.16), channel_id=1, source_target_pairs={{0,1},{1,0},{2,3},{3,2},{4,5},{5,4},{6,7},{7,6},{8,9},{9,8},{10,11... | collective-permute-start | bytes 3145736 | tf_op jit(solution)/shard_map/ppermute | solution.py:445

commit v3 on v2

v3 whole, which is shorter than its diff:
```python
import jax
import jax.numpy as jnp
from jax import lax
from jax.experimental import pallas as pl
from jax.experimental.pallas import tpu as pltpu
from jax.sharding import PartitionSpec as P

HIGH = lax.Precision.HIGHEST
F32 = jnp.float32
OUTER = 32


def dot_lead(left, right):
    return lax.dot_general(left, right, (((0,), (0,)), ((), ())), precision=HIGH, preferred_element_type=F32)


def dot_last(left, right):
    return lax.dot_general(left, right, (((1,), (1,)), ((), ())), precision=HIGH, preferred_element_type=F32)


def splat_lane(tile, lane):
    return jnp.broadcast_to(tile[:, lane:lane + 1], (8, 128))


def splat_row(tile, row):
    return jnp.broadcast_to(tile[row:row + 1, :], (8, 128))


def split3(value):
    high = value.astype(jnp.bfloat16)
    rest = value - high.astype(F32)
    middle = rest.astype(jnp.bfloat16)
    low = (rest - middle.astype(F32)).astype(jnp.bfloat16)
    return high, middle, low


def dot_bf16(left, right, dims):
    return lax.dot_general(left, right, (dims, ((), ())), preferred_element_type=F32)


STACK_A, STACK_B = (0, 0, 0, 1, 1, 2), (0, 1, 2, 0, 1, 0)


def factor_inverse(work, upper, outer):
    n = work.shape[0]
    tiles = n // 128
    count = outer // 8
    sub = lax.broadcasted_iota(jnp.int32, (8, 128), 0)
    lane = lax.broadcasted_iota(jnp.int32, (8, 128), 1)
    here = work[0:outer, :]
    for r0 in range(0, n, outer):
        panel = [[here[8 * t:8 * t + 8, 128 * c:128 * c + 128] for c in range(tiles)] for t in range(count)]
        uppers, lowers = [], []
        for b in range(count):
            r = r0 + 8 * b
            own, base = r // 128, r % 128
            cols = {t: [splat_lane(panel[t][own], base + j) for j in range(8)] for t in range(b, count)}
            d = [[splat_row(cols[b][j], i) if i >= j else None for j in range(8)] for i in range(8)]
            inv = [None] * 8
            low = [[None] * 8 for _ in range(8)]
            for j in range(8):
                inv[j] = lax.rsqrt(d[j][j])
                for i in range(j + 1, 8):
                    low[i][j] = d[i][j] * inv[j]
                for i in range(j + 1, 8):
                    for k in range(j + 1, i + 1):
                        d[i][k] = d[i][k] - low[i][j] * low[k][j]
            mine = (lane >= base) & (lane < base + 8)
            cleared = jnp.where(mine, jnp.where(lane - base == sub, 1.0, 0.0), panel[b][own])
            sources = [panel[b][c] if c != own else cleared for c in range(tiles)] + [panel[b][own]]
            rows = [[splat_row(src, j) for src in sources] for j in range(8)]
            for j in range(8):
                for s in range(tiles + 1):
                    acc = rows[j][s]
                    for k in range(j):
                        acc = acc - low[j][k] * rows[k][s]
                    rows[j][s] = acc * inv[j]
            for t in range(b + 1, count):
                below = []
                for j in range(8):
                    acc = cols[t][j]
                    for k in range(j):
                        acc = acc - below[k] * low[j][k]
                    below.append(acc * inv[j])
                for c in range(tiles):
                    acc = panel[t][c]
                    if c == own:
                        acc = jnp.where(mine, 0.0, acc)
                    for j in range(8):
                        acc = acc - below[j] * rows[j][c]
                    panel[t][c] = acc
            done = []
            for s in range(tiles + 1):
                tile = rows[0][s]
                for j in range(1, 8):
                    tile = jnp.where(sub == j, rows[j][s], tile)
                done.append(tile)
            up, down = [], []
            for c in range(tiles):
                work[r:r + 8, 128 * c:128 * c + 128] = done[c]
                at = lane + 128 * c - r
                if c < own:
                    up.append(jnp.zeros((8, 128), F32))
                elif c == own:
                    up.append(jnp.where(lane >= base + sub, done[tiles], 0.0))
                else:
                    up.append(done[c])
                upper[r:r + 8, 128 * c:128 * c + 128] = up[c]
                down.append(jnp.where((at >= 8) & (at < outer - 8 * b), 0.0, done[c]) if c == own else done[c])
            uppers.append(jnp.concatenate(up, axis=1))
            lowers.append(jnp.concatenate(down, axis=1))
        after = r0 + outer
        if after < n:
            up, down = split3(jnp.concatenate(uppers, axis=0)), split3(jnp.concatenate(lowers, axis=0))
            left = jnp.concatenate([up[k] for k in STACK_A[::-1]], axis=0)
            right = jnp.concatenate([down[k] for k in STACK_B[::-1]], axis=0)
            start = after // 128 * 128

            def left_over(begin, end, first, last):
                change = dot_bf16(left[:, first:last], right, ((0,), (0,)))[begin - first:end - first]
                col = lax.broadcasted_iota(jnp.int32, (end - begin, n), 1)
                return jnp.where((col >= r0) & (col < after), 0.0, work[begin:end, :]) - change

            here = left_over(after, after + outer, start, start + 128)
            if after + outer < n:
                work[after + outer:n, :] = left_over(after + outer, n, start, n)


def gram_of(parts):
    high, middle, low = parts
    lead = ((0,), (0,))
    cross = dot_bf16(high, middle, lead) + dot_bf16(high, low, lead)
    return dot_bf16(middle, middle, lead) + (cross + cross.T) + dot_bf16(high, high, lead)


def times_transposed(parts, right):
    high, middle, low = parts
    r_high, r_middle, r_low = split3(right)
    left = jnp.concatenate([low, middle, high, middle, high, high], axis=1)
    other = jnp.concatenate([r_high, r_middle, r_low, r_high, r_middle, r_high], axis=1)
    return dot_bf16(left, other, ((1,), (1,)))


def dot_three(left, right, dims):
    l_high, l_middle, _ = split3(left)
    r_high, r_middle, _ = split3(right)
    small = dot_bf16(l_high, r_middle, dims) + dot_bf16(l_middle, r_high, dims)
    return small + dot_bf16(l_high, r_high, dims)


NEAR = 0.0025


def tail_kernel(where_ref, mine_ref, other_ref, basis_ref, factor_ref, gram_ref, held, work, upper, first_upper):
    n = work.shape[0]
    rows = basis_ref.shape[0]
    part = mine_ref.shape[0]
    total = float(2 * part)
    scale = total ** 0.5
    lane = where_ref[0]
    held[pl.ds(pl.multiple_of(lane * part, part), part), :] = mine_ref[...]
    held[pl.ds(pl.multiple_of((1 - lane) * part, part), part), :] = other_ref[...]
    row = lax.broadcasted_iota(jnp.int32, (n, n), 0)
    col = lax.broadcasted_iota(jnp.int32, (n, n), 1)
    identity = jnp.where(row == col, 1.0, 0.0)
    at = pl.multiple_of(where_ref[1], 16)
    gram1 = gram_of(split3(held[...]))
    gram_ref[...] = gram1 / total
    work[...] = gram1

    def one_pass(state):
        step, _ = state
        factor_inverse(work, upper, OUTER)

        def after_first():
            first_upper[...] = upper[...]
            inverse = jnp.where(col <= row, work[...], 0.0)
            first = times_transposed(split3(held[...]), inverse)
            held[...] = first
            gram2 = gram_of(split3(first))
            work[...] = gram2
            error = gram2 - identity
            return jnp.where(jnp.sum(error * error) <= NEAR, 0, 1)

        again = lax.cond(step == 0, after_first, lambda: 0)
        return step + 1, again

    passes, _ = lax.while_loop(lambda state: state[1] > 0, one_pass, (0, 1))

    @pl.when(passes == 1)
    def _():
        error = work[...] - identity
        weight = jnp.where(col < row, 1.0, jnp.where(col == row, 0.5, 0.0))
        extra = error * weight
        for _ in range(2):
            extra = (error - dot_three(extra, extra, ((1,), (1,)))) * weight
        square = dot_three(extra, extra, ((1,), (0,)))
        value = held[pl.ds(at, rows), :]
        value = value - dot_last(value, extra)
        value = value + dot_last(value, square)
        basis_ref[...] = value * scale
        factor_ref[...] = (first_upper[...] + dot_lead(extra, first_upper[...])) / scale

    @pl.when(passes != 1)
    def _():
        inverse = jnp.where(col <= row, work[...], 0.0)
        basis_ref[...] = dot_last(held[pl.ds(at, rows), :], inverse) * scale
        factor_ref[...] = jnp.dot(upper[...], first_upper[...], precision=HIGH, preferred_element_type=F32) / scale


def tail(mine, other, where, rows):
    part, n = mine.shape
    vmem = pl.BlockSpec(memory_space=pltpu.VMEM)
    return pl.pallas_call(
        tail_kernel,
        out_shape=(
            jax.ShapeDtypeStruct((rows, n), F32),
            jax.ShapeDtypeStruct((n, n), F32),
            jax.ShapeDtypeStruct((n, n), F32),
        ),
        in_specs=[pl.BlockSpec(memory_space=pltpu.SMEM), vmem, vmem],
        out_specs=(vmem, vmem, vmem),
        scratch_shapes=[
            pltpu.VMEM((2 * part, n), F32),
            pltpu.VMEM((n, n), F32),
            pltpu.VMEM((n, n), F32),
            pltpu.VMEM((n, n), F32),
        ],
        compiler_params=pltpu.CompilerParams(vmem_limit_bytes=24 * 1024 * 1024),
    )(where, mine, other)


SIDE = 4
STRIDE = {"x": 16, "z": 4, "y": 1}
ORDERS = ("xy", "yx", "zy")
SWAP = [(0, 1), (1, 0)]


def whole(*shape):
    return pl.BlockSpec(shape, lambda *_: (0,) * len(shape))


def image_blocks(x_long, x_short, y_long, y_short, test, outs):
    short = outs[2].shape[1] // 2

    def image(left, weight, out):
        value = jnp.dot(left[...], test[...], preferred_element_type=F32) * weight
        return value.reshape(out.shape[0], -1, out.shape[2])

    third = [image(x_short, 2.0, outs[2]), image(y_short, -1.0, outs[2])]
    return image(x_long, 2.0, outs[0]), image(y_long, -1.0, outs[1]), jnp.concatenate(third, axis=1)


def send_kernel(half, test, x_long, x_short, y_long, y_short, *outs):
    for value, out in zip(image_blocks(x_long, x_short, y_long, y_short, test, outs), outs):
        out[...] = value


def keep_kernel(half, test, x_long, x_short, y_long, y_short, *refs):
    came, give, keep = refs[:3], refs[3:6], refs[6:]
    step = pl.program_id(0)
    values = image_blocks(x_long, x_short, y_long, y_short, test, give)
    for part in range(3):
        value = values[part] + came[part][...]

        @pl.when(step < pl.num_programs(0) // 2)
        def _():
            give[part][...] = value

        @pl.when(step >= pl.num_programs(0) // 2)
        def _():
            keep[part][...] = value


def image_call(halves, exchange, direct, test, steps, came=None):
    depth, width = exchange.shape
    rank = test.shape[1]
    slices = SIDE * SIDE
    long, short = 3 * depth // (4 * slices), depth // (4 * slices)
    per = slices // 2 // steps
    skip = slices * long // (per * short)
    middle = steps // 2

    def block(i, halves, part):
        if came is None:
            return i
        near = halves[3 + part]
        return jnp.where(i < middle, (1 - near) * middle + i, near * middle + i - middle)

    def left(rows, part, skip):
        return pl.BlockSpec((rows, width), lambda i, halves: (skip + halves[part] * steps + block(i, halves, part), 0))

    sizes = [long, long, 2 * short]
    in_specs = [
        whole(width, rank), left(per * long, 0, 0), left(per * short, 2, skip),
        left(per * long, 1, 0), left(per * short, 2, skip),
    ]
    operands = [halves, test, exchange, exchange, direct, direct]
    if came is None:
        out_specs = [pl.BlockSpec((per, size, rank), lambda i, halves: (i, 0, 0)) for size in sizes]
        shapes = [(slices // 2, size, rank) for size in sizes]
    else:
        for part, size in enumerate(sizes):
            in_specs.append(pl.BlockSpec(
                (per, size, rank), lambda i, halves, part=part: (block(i, halves, part), 0, 0)
            ))
        operands += came
        out_specs = [
            pl.BlockSpec((per, size, rank), lambda i, halves: (jnp.minimum(i, middle - 1), 0, 0)) for size in sizes
        ] + [
            pl.BlockSpec((per, size, rank), lambda i, halves: (jnp.maximum(i - middle, 0), 0, 0)) for size in sizes
        ]
        shapes = [(slices // 4, size, rank) for size in sizes] * 2
    return list(pl.pallas_call(
        send_kernel if came is None else keep_kernel,
        grid_spec=pltpu.PrefetchScalarGridSpec(
            num_scalar_prefetch=1, grid=(steps,), in_specs=in_specs, out_specs=out_specs
        ),
        out_shape=[jax.ShapeDtypeStruct(shape, F32) for shape in shapes],
        compiler_params=pltpu.CompilerParams(vmem_limit_bytes=56 * 1024 * 1024 if came is None else 56 * 1024 * 1024),
    )(*operands))


def rows_kernel(picks_row, energy_row, test, x_long, x_short, y_long, y_short, packed, diagonal, chosen, held):
    width = test.shape[0]
    count = picks_row.shape[1]
    together = packed.shape[2]
    long, short = 3 * together // 8, together // 8
    per = x_long.shape[0] // long
    step = pl.program_id(0)

    @pl.when(step == 0)
    def _():
        spot = lax.broadcasted_iota(jnp.int32, (width, count), 0) == picks_row[...]
        chosen[...] = jnp.where(spot, 1.0, 0.0).astype(jnp.bfloat16)
        column = jnp.broadcast_to(picks_row[...].astype(F32), (count, count)).T[:, :1].astype(jnp.int32)
        here = lax.broadcasted_iota(jnp.int32, (count, width), 1) == column
        energy = jnp.sum(jnp.where(here, energy_row[...], 0.0), axis=1, keepdims=True)
        taken = jnp.dot(here.astype(F32).astype(jnp.bfloat16), test[...], preferred_element_type=F32)
        diagonal[...] = energy * taken

    def own(left):
        return jnp.dot(left[...], chosen[...], preferred_element_type=F32).T

    first, second, x_third, y_third = own(x_long), own(y_long), own(x_short), own(y_short)
    blank = lambda size: jnp.zeros((count, size), F32)
    for low in range(per):
        at = step * per + low
        long_cut, short_cut = slice(low * long, (low + 1) * long), slice(low * short, (low + 1) * short)
        held[0, at] = jnp.concatenate([first[:, long_cut], blank(long + 2 * short)], axis=1)
        held[1, at] = jnp.concatenate([blank(long + 2 * short), second[:, long_cut]], axis=1)
        held[2, at] = jnp.concatenate(
            [blank(long), x_third[:, short_cut], y_third[:, short_cut], blank(long)], axis=1
        )

    @pl.when(step == pl.num_programs(0) - 1)
    def _():
        for x in range(SIDE):
            for z in range(SIDE):
                for y in range(SIDE):
                    cell = x * STRIDE["x"] + z * STRIDE["z"] + y * STRIDE["y"]
                    value = held[0, x * SIDE + y] + held[1, y * SIDE + x] + held[2, z * SIDE + y]
                    packed[cell] = value.astype(jnp.bfloat16)


def rows_call(exchange, direct, test, energies, picks):
    depth, width = exchange.shape
    rank = test.shape[1]
    count = picks.shape[1]
    cells = SIDE ** 3
    slices = SIDE * SIDE
    long, short = 3 * depth // (4 * slices), depth // (4 * slices)
    together = 2 * (long + short)
    steps = 1
    long_block = pl.BlockSpec((slices // steps * long, width), lambda i: (i, 0))
    short_block = pl.BlockSpec((slices // steps * short, width), lambda i: (3 * steps + i, 0))
    return pl.pallas_call(
        rows_kernel,
        grid=(steps,),
        in_specs=[
            whole(1, count), whole(1, width), whole(width, rank),
            long_block, short_block, long_block, short_block,
        ],
        out_specs=[whole(cells, count, together), whole(count, rank)],
        out_shape=[
            jax.ShapeDtypeStruct((cells, count, together), jnp.bfloat16),
            jax.ShapeDtypeStruct((count, rank), F32),
        ],
        scratch_shapes=[
            pltpu.VMEM((width, count), jnp.bfloat16),
            pltpu.VMEM((3, slices, count, together), F32),
        ],
        compiler_params=pltpu.CompilerParams(vmem_limit_bytes=56 * 1024 * 1024),
    )(picks, energies.reshape(1, width), test, exchange, exchange, direct, direct)


def couple_kernel(first, second, away, own_rows, other_rows, out):
    cells, half_rows, together = own_rows.shape
    image = jnp.concatenate([first[0], second[0]], axis=0)
    total = jnp.zeros((cells * half_rows, image.shape[1]), F32)
    pieces = [(other_rows, piece) for piece in split3(away[...])] + [(own_rows, piece) for piece in split3(image)]
    for rows, piece in (pieces[2], pieces[5], pieces[1], pieces[4], pieces[0], pieces[3]):
        left = rows[...].reshape(cells * half_rows, together)
        total = total + jnp.dot(left, piece, preferred_element_type=F32)
    out[...] = total.reshape(out.shape)


def couple(parts, away, own_rows, other_rows):
    cells, half_rows, _ = own_rows.shape
    vmem = pl.BlockSpec(memory_space=pltpu.VMEM)
    return pl.pallas_call(
        couple_kernel,
        out_shape=jax.ShapeDtypeStruct((cells, half_rows, away.shape[1]), F32),
        in_specs=[vmem] * 5,
        out_specs=vmem,
        compiler_params=pltpu.CompilerParams(vmem_limit_bytes=16 * 1024 * 1024),
    )(*parts, away, own_rows, other_rows)


def neighbours(axis, far):
    pairs = []
    for device in range(SIDE ** 3):
        at = device // STRIDE[axis] % SIDE
        to = SIDE - 1 - at if far else at ^ 1
        pairs.append((device, device + (to - at) * STRIDE[axis]))
    return pairs


def shards(exchange_pairs, direct_pairs, test_matrix, energies, picks):
    cells = lax.axis_size("col")
    lane = lax.axis_index("pw")
    place = lax.axis_index("col")
    at = {axis: place // STRIDE[axis] % SIDE for axis in "xyz"}
    far = jnp.stack([at[order[0]] // 2 for order in ORDERS]).astype(jnp.int32)
    near = jnp.stack([at[order[0]] % 2 for order in ORDERS]).astype(jnp.int32)
    gives = image_call(1 - far, exchange_pairs, direct_pairs, test_matrix, 2)
    picks, gives = lax.optimization_barrier((picks, gives))
    came = [lax.ppermute(give, "col", neighbours(order[0], True)) for give, order in zip(gives, ORDERS)]
    packed, diagonal = rows_call(exchange_pairs, direct_pairs, test_matrix, energies, picks)
    bits, packed, diagonal = lax.optimization_barrier((jnp.concatenate([far, near]), packed, diagonal))
    made = image_call(bits, exchange_pairs, direct_pairs, test_matrix, 2, came)
    packed = lax.all_to_all(packed, "col", split_axis=0, concat_axis=0, tiled=True)
    gives, keeps = lax.optimization_barrier(made[:3]), made[3:]
    keeps = [keep + lax.ppermute(give, "col", neighbours(order[0], False))
             for keep, give, order in zip(keeps, gives, ORDERS)]
    keeps = [jnp.concatenate([keeps[0], keeps[2]], axis=1), keeps[1]]
    for bit_of in (lambda v: v // 2, lambda v: v % 2):
        gives = []
        for part, order in enumerate(ORDERS[:2]):
            value = keeps[part]
            size = value.shape[0] // 2
            bit = bit_of(at[order[1]])
            gives.append(lax.dynamic_slice_in_dim(value, (1 - bit) * size, size, 0))
            keeps[part] = lax.dynamic_slice_in_dim(value, bit * size, size, 0)
        if size > 1:
            gives, packed, diagonal = lax.optimization_barrier((gives, packed, diagonal))
            half = packed.shape[1] // 2
            own_rows = lax.dynamic_slice_in_dim(packed, lane * half, half, 1)
            other_rows = lax.ppermute(lax.dynamic_slice_in_dim(packed, (1 - lane) * half, half, 1), "pw", SWAP)
        else:
            gives = lax.optimization_barrier(gives)
        for part, order in enumerate(ORDERS[:2]):
            keeps[part] = keeps[part] + lax.ppermute(gives[part], "col", neighbours(order[1], size > 1))
    away = lax.ppermute(jnp.concatenate([keep[0] for keep in keeps], axis=0), "pw", SWAP)
    both = couple(keeps, away, own_rows, other_rows)
    own_diagonal = lax.dynamic_slice_in_dim(diagonal, lane * half, half, 0)
    where = jnp.stack([lane, lane * (cells * half) + place * half]).astype(jnp.int32)
    both, own_diagonal, where = lax.optimization_barrier((both, own_diagonal, where))
    arrived = lax.all_to_all(both, "col", split_axis=0, concat_axis=0, tiled=True)
    sketch = jnp.sum(arrived, axis=0) + own_diagonal
    copies = jnp.broadcast_to(sketch[None], (cells,) + sketch.shape)
    mine = lax.all_to_all(copies, "col", split_axis=0, concat_axis=0, tiled=True)
    other = lax.ppermute(mine, "pw", SWAP)
    rank = sketch.shape[1]
    basis, factor, gram = tail(mine.reshape(cells * half, rank), other.reshape(cells * half, rank), where, half)
    return (sketch, basis, factor, gram)


def solution(mesh):
    return jax.shard_map(
        shards,
        mesh=mesh,
        in_specs=(P("pw", "col"), P("pw", "col"), P("col", None), P("col"), P("col", None)),
        out_specs=(P(("col", "pw"), None), P(("col", "pw"), None), P(), P()),
        check_vma=False,
    )
```

time: 151 us -> 147 us (0.974)
  waiting for transfers between devices: 16 us -> 26.7 us
  Pallas kernels: 41.8 us -> 35.8 us
  starting transfers between devices: 33.8 us -> 28.1 us
  local copies, waits for them, and re-layouts: 7.48 us -> 3.07 us
  blocking collectives: 46 us -> 48.2 us
    ppermute x10 -> x9, waiting for transfers between devices: 13.7 us -> 24 us  [the longest x4 12.5 us: shards(): lax.ppermute(gives[part], 'col', neighbours(order[1], size > 1))]
    ppermute x10 -> x9, starting transfers between devices: 16.1 us -> 10.4 us  [the longest x3 3.48 us: shards(): lax.ppermute(give, 'col', neighbours(order[0], False))]
    pallas_call x5 -> x4, Pallas kernels: 22.7 us -> 18.6 us  [the longest x2 10.8 us: image_call(): pl.pallas_call(send_kernel if came is None else keep_kernel, grid_spec=pl...]
    unnamed x16 -> x12, local copies, waits for them, and re-layouts: 4.75 us -> 1.58 us
    all_to_all x1, blocking collectives: 24.4 us -> 26.6 us  [shards(): lax.all_to_all(both, 'col', split_axis=0, concat_axis=0, tiled=True)]
    add x9 -> x4, other arithmetic: 2.19 us -> 0.1 us  [shards(): keeps[part]]
    pallas_call x1, Pallas kernels: 19.1 us -> 17.2 us  [tail(): pl.pallas_call(tail_kernel, out_shape=(jax.ShapeDtypeStruct((rows, n), F3...]
    add x1 -> x3, other arithmetic: 1.43 us -> 3.08 us  [shards(): keep + lax.ppermute(give, 'col', neighbours(order[0], False))]
  transfers between devices with their start and end apart: 15 -> 14, of which waited for: 9 -> 7; matrix products, arithmetic and copies ran while one was open for 3% -> 3% of each run, Pallas kernels for 10% -> 9%
where the time goes in v3:
time: 147 us
  blocking collectives  48.2 us (33%)
  Pallas kernels  35.8 us (24%)
  starting transfers between devices  28.1 us (19%)
  waiting for transfers between devices  26.7 us (18%)
  other arithmetic  4 us (3%)
  local copies, waits for them, and re-layouts  3.07 us (2%)
    all_to_all x1, blocking collectives, shards(): lax.all_to_all(both, 'col', split_axis=0, concat_axis=0, tiled=True)  26.6 us
    all_to_all x1, blocking collectives, shards(): lax.all_to_all(copies, 'col', split_axis=0, concat_axis=0, tiled=True)  21.6 us
    pallas_call x1, Pallas kernels, tail(): pl.pallas_call(tail_kernel, out_shape=(jax.ShapeDtypeStruct((rows, n), F3...  17.2 us
    ppermute x4, waiting for transfers between devices, shards(): lax.ppermute(gives[part], 'col', neighbours(order[1], size > 1))  12.5 us
    pallas_call x2, Pallas kernels, image_call(): pl.pallas_call(send_kernel if came is None else keep_kernel, grid_spec=pl...  10.8 us
    ppermute x3, waiting for transfers between devices, shards(): lax.ppermute(give, 'col', neighbours(order[0], False))  10.4 us
    ppermute x3, starting transfers between devices, shards(): lax.ppermute(give, 'col', neighbours(order[0], True))  9.8 us
    pallas_call x1, Pallas kernels, rows_call(): pl.pallas_call(rows_kernel, grid=(steps,), in_specs=[whole(1, count), who...  6.89 us
  transfers between devices with their start and end apart: 14, of which 7 were waited for; matrix products, arithmetic and copies ran while one was open for 3% of the time, Pallas kernels for 9%

profile of v3, /device:TPU:1, one launch (start us, length us, event | category | flops | bytes accessed | tf_op | source)
XLA Modules:
  0.0 146.8 jit_solution(15670991755627231913)
XLA Ops:
  0.8 0.6 add_subtract_fusion.half
  1.3 0.0 copy-start.5
  1.3 4.9 %shard_map.84 = (f32[8,96,256]{2,1,0:T(8,128)}, f32[8,96,256]{2,1,0:T(8,128)}, f32[8,64,256]{2,1,0:T(8,128)}) custom-call(s32[3]{0:T(128)} %add_subtract_fusion.half, bf16[896,256]{1,0:T(8,128)(2,1)} %test.5, bf16[2048,896]{1,0:T(8,128)(2,1)} %x_short.5, bf16[2048,896]{1,0:T(8,128)(2,1)} %x_short.5, bf16[2048,896]{1,0:T(8,128)(2,1)} %y_short.5, ...), custom_call_target="tpu_custom_call" | custom-call | tf_op jit(solution)/shard_map/pallas_call | solution.py:314
  6.3 3.3 %collective-permute-start = (f32[8,96,256]{2,1,0:T(8,128)}, f32[8,96,256]{2,1,0:T(8,128)S(1)}, u32[]{:S(2)}, u32[]{:S(2)}) collective-permute-start(f32[8,96,256]{2,1,0:T(8,128)} %get-tuple-element.44), channel_id=1, source_target_pairs={{0,96},{2,98},{4,100},{6,102},{8,104},{10,106},{12,108},{14,110},{... | collective-permute-start | bytes 2359304 | tf_op jit(solution)/shard_map/ppermute | solution.py:438
  9.6 2.7 %collective-permute-start.1 = (f32[8,96,256]{2,1,0:T(8,128)}, f32[8,96,256]{2,1,0:T(8,128)S(1)}, u32[]{:S(2)}, u32[]{:S(2)}) collective-permute-start(f32[8,96,256]{2,1,0:T(8,128)} %get-tuple-element.45), channel_id=1, source_target_pairs={{0,6},{2,4},{4,2},{6,0},{8,14},{10,12},{12,10},{14,8},{16,22},{18,... | collective-permute-start | bytes 2359304 | tf_op jit(solution)/shard_map/ppermute | solution.py:438
  12.3 3.7 %collective-permute-start.2 = (f32[8,64,256]{2,1,0:T(8,128)}, f32[8,64,256]{2,1,0:T(8,128)S(1)}, u32[]{:S(2)}, u32[]{:S(2)}) collective-permute-start(f32[8,64,256]{2,1,0:T(8,128)} %get-tuple-element.46), channel_id=1, source_target_pairs={{0,24},{2,26},{4,28},{6,30},{8,16},{10,18},{12,20},{14,22},{16,8},... | collective-permute-start | bytes 1572872 | tf_op jit(solution)/shard_map/ppermute | solution.py:438
  16.1 0.0 copy-done.5
  16.1 0.6 reshape.18.energy_row
  16.7 6.9 %shard_map.85 = (bf16[64,32,256]{2,1,0:T(8,128)(2,1)}, f32[32,256]{1,0:T(8,128)}) custom-call(s32[1,32]{1,0:T(1,128)} %picks_row, f32[1,896]{1,0:T(1,128)} %reshape.18.energy_row, bf16[896,256]{1,0:T(8,128)(2,1)} %test.5, bf16[2048,896]{1,0:T(8,128)(2,1)} %x_short.5, bf16[2048,896]{1,0:T(8,128)(2,1)} %x_short.5, bf16[2048,896]{1,0:T(8,128)(2,1)} %y_short.5, ...), custom_call_target="tpu_custom_call" | custom-call | tf_op jit(solution)/shard_map/pallas_call | solution.py:377
  23.6 0.6 concatenate.10.half
  24.2 4.7 %all-to-all-start = ((bf16[64,32,256]{2,1,0:T(8,128)(2,1)}), bf16[64,32,256]{2,1,0:T(8,128)(2,1)S(1)}, u32[]{:S(2)}, u32[]{:S(2)}) async-start(bf16[64,32,256]{2,1,0:T(8,128)(2,1)} %get-tuple-element.56), calls=%async_computation | async-start | bytes 2097152 | tf_op jit(solution)/shard_map/all_to_all | solution.py:442
  28.8 0.0 collective-permute-done.2.refs_2_
  28.9 0.0 copy-start.2
  28.9 0.0 collective-permute-done.refs_0_
  28.9 0.0 copy-start
  28.9 0.4 collective-permute-done.1.refs_1_
  29.3 0.4 copy-done.2
  29.6 0.3 copy-done
  29.9 0.0 copy-start.1
  29.9 0.9 copy-done.1
  30.8 5.8 %shard_map.86 = (f32[4,96,256]{2,1,0:T(8,128)}, f32[4,96,256]{2,1,0:T(8,128)}, f32[4,64,256]{2,1,0:T(8,128)}, f32[4,96,256]{2,1,0:T(8,128)}, f32[4,96,256]{2,1,0:T(8,128)}, /*index=5*/f32[4,64,256]{2,1,0:T(8,128)}) custom-call(s32[6]{0:T(128)} %concatenate.10.half, bf16[896,256]{1,0:T(8,128)(2,1)} %test.5, bf16[2048,896]{1,0:T(8,128)(2,1)} %x_short.5, ...), custom_call_target="tpu_custom_call" | custom-call | tf_op jit(solution)/shard_map/pallas_call | solution.py:314
  36.6 1.0 collective-permute-start.5
  37.6 1.3 collective-permute-start.3
  38.9 1.2 collective-permute-start.4
  40.1 10.4 %collective-permute-done.4 = f32[4,64,256]{2,1,0:T(8,128)S(1)} collective-permute-done((f32[4,64,256]{2,1,0:T(8,128)}, f32[4,64,256]{2,1,0:T(8,128)S(1)}, u32[]{:S(2)}, u32[]{:S(2)}) %collective-permute-start.4) | collective-permute-done | bytes 262176 | tf_op jit(solution)/shard_map/ppermute | solution.py:444
  50.5 1.0 add.94
  51.5 0.0 collective-permute-done.5
  51.5 1.0 add.97
  52.6 0.0 collective-permute-done.3
  52.6 1.0 add.93
  53.7 0.0 copy-start.4
  53.7 0.0 all-to-all-done
  53.7 0.5 collective-permute-start.7
  54.3 2.0 %collective-permute-start.6 = (f32[2,160,256]{2,1,0:T(8,128)S(1)}, f32[2,160,256]{2,1,0:T(8,128)S(1)}, u32[]{:S(2)}, u32[]{:S(2)}) collective-permute-start(f32[2,160,256]{2,1,0:T(8,128)S(1)} %fusion), channel_id=1, source_target_pairs={{0,6},{2,4},{4,2},{6,0},{8,14},{10,12},{12,10},{14,8},{16,22},{18,... | collective-permute-start | bytes 983048 | tf_op jit(solution)/shard_map/ppermute | solution.py:463
  56.3 4.7 %collective-permute-done.7 = f32[2,96,256]{2,1,0:T(8,128)S(1)} collective-permute-done((f32[2,96,256]{2,1,0:T(8,128)S(1)}, f32[2,96,256]{2,1,0:T(8,128)S(1)}, u32[]{:S(2)}, u32[]{:S(2)}) %collective-permute-start.7) | collective-permute-done | bytes 196640 | tf_op jit(solution)/shard_map/ppermute | solution.py:463
  61.1 2.0 %collective-permute-done.6 = f32[2,160,256]{2,1,0:T(8,128)S(1)} collective-permute-done((f32[2,160,256]{2,1,0:T(8,128)S(1)}, f32[2,160,256]{2,1,0:T(8,128)S(1)}, u32[]{:S(2)}, u32[]{:S(2)}) %collective-permute-start.6) | collective-permute-done | bytes 327712 | tf_op jit(solution)/shard_map/ppermute | solution.py:463
  63.2 0.8 collective-permute-start.9
  64.0 0.1 constant_dynamic-slice_fusion.1
  64.1 2.6 %collective-permute-start.11 = (bf16[64,16,256]{2,1,0:T(8,128)(2,1)S(1)}, bf16[64,16,256]{2,1,0:T(8,128)(2,1)S(1)}, u32[]{:S(2)}, u32[]{:S(2)}) collective-permute-start(bf16[64,16,256]{2,1,0:T(8,128)(2,1)S(1)} %get-tuple-element.70), channel_id=1, source_target_pairs={{0,1},{1,0},{2,3},{3,2},{4,5},{5,4},{6,7},{7,6},{8,9},{9,8},{10,11... | collective-permute-start | bytes 1572872 | tf_op jit(solution)/shard_map/ppermute | solution.py:459
  66.7 0.0 collective-permute-start.8
  66.7 0.0 collective-permute-done.9
  66.7 5.7 %collective-permute-done.8 = f32[1,160,256]{2,1,0:T(8,128)S(1)} collective-permute-done((f32[1,160,256]{2,1,0:T(8,128)S(1)}, f32[1,160,256]{2,1,0:T(8,128)S(1)}, u32[]{:S(2)}, u32[]{:S(2)}) %collective-permute-start.8) | collective-permute-done | bytes 163872 | tf_op jit(solution)/shard_map/ppermute | solution.py:463
  72.5 1.0 collective-permute-start.10
  73.4 0.1 pad_add_fusion.where_ref
  73.5 0.0 copy-done.4
  73.5 0.0 collective-permute-done.11.other_rows
  73.5 1.1 collective-permute-done.10.away
  74.6 1.0 shard_map.87
  75.6 26.6 %all_to_all.15 = f32[64,16,256]{2,1,0:T(8,128)S(1)} all-to-all(f32[64,16,256]{2,1,0:T(8,128)S(1)} %shard_map.87), channel_id=1, replica_groups=mesh['col'=64,'pw'=2] {'col'}, dimensions={0} | all-to-all | bytes 2097152 | tf_op jit(solution)/shard_map/all_to_all | solution.py:469
  102.1 0.1 reduce_sum.9
  102.3 0.0 copy-start.3
  102.3 0.1 broadcast_in_dim.2
  102.4 21.6 %all_to_all.16 = f32[64,16,256]{2,1,0:T(8,128)S(1)} all-to-all(f32[64,16,256]{2,1,0:T(8,128)S(1)} %broadcast_in_dim.2), channel_id=1, replica_groups=mesh['col'=64,'pw'=2] {'col'}, dimensions={0} | all-to-all | bytes 2097152 | tf_op jit(solution)/shard_map/all_to_all | solution.py:472
  124.0 3.3 %collective-permute-start.12 = (f32[64,16,256]{2,1,0:T(8,128)S(1)}, f32[64,16,256]{2,1,0:T(8,128)S(1)}, u32[]{:S(2)}, u32[]{:S(2)}) collective-permute-start(f32[64,16,256]{2,1,0:T(8,128)S(1)} %all_to_all.16), channel_id=1, source_target_pairs={{0,1},{1,0},{2,3},{3,2},{4,5},{5,4},{6,7},{7,6},{8,9},{9,8},{10,11... | collective-permute-start | bytes 3145736 | tf_op jit(solution)/shard_map/ppermute | solution.py:473
  127.3 2.3 %collective-permute-done.12 = f32[64,16,256]{2,1,0:T(8,128)S(1)} collective-permute-done((f32[64,16,256]{2,1,0:T(8,128)S(1)}, f32[64,16,256]{2,1,0:T(8,128)S(1)}, u32[]{:S(2)}, u32[]{:S(2)}) %collective-permute-start.12) | collective-permute-done | bytes 1048608 | tf_op jit(solution)/shard_map/ppermute | solution.py:473
  129.6 17.2 %shard_map.88 = (f32[16,256]{1,0:T(8,128)}, f32[256,256]{1,0:T(8,128)}, f32[256,256]{1,0:T(8,128)}) custom-call(s32[2]{0:T(128)S(1)} %pad_add_fusion.where_ref, f32[1024,256]{1,0:T(8,128)S(1)} %bitcast.12, f32[1024,256]{1,0:T(8,128)S(1)} %bitcast.14), custom_call_target="tpu_custom_call" | custom-call | tf_op jit(solution)/shard_map/pallas_call | solution.py:214
  146.8 0.0 copy-done.3
  (11 shorter events, 0.2 us)
Async XLA Ops:
  1.3 14.7 %copy-start.5 = (f32[896]{0:T(1024)S(1)}, f32[896]{0:T(1024)}, u32[]{:S(2)}) copy-start(f32[896]{0:T(1024)} %param.8) | copy-start | bytes 10756
  6.3 22.6 %collective-permute-start = (f32[8,96,256]{2,1,0:T(8,128)}, f32[8,96,256]{2,1,0:T(8,128)S(1)}, u32[]{:S(2)}, u32[]{:S(2)}) collective-permute-start(f32[8,96,256]{2,1,0:T(8,128)} %get-tuple-element.44), channel_id=1, source_target_pairs={{0,96},{2,98},{4,100},{6,102},{8,104},{10,106},{12,108},{14,110},{... | collective-permute-start | bytes 2359304 | tf_op jit(solution)/shard_map/ppermute | solution.py:438
  9.6 19.7 %collective-permute-start.1 = (f32[8,96,256]{2,1,0:T(8,128)}, f32[8,96,256]{2,1,0:T(8,128)S(1)}, u32[]{:S(2)}, u32[]{:S(2)}) collective-permute-start(f32[8,96,256]{2,1,0:T(8,128)} %get-tuple-element.45), channel_id=1, source_target_pairs={{0,6},{2,4},{4,2},{6,0},{8,14},{10,12},{12,10},{14,8},{16,22},{18,... | collective-permute-start | bytes 2359304 | tf_op jit(solution)/shard_map/ppermute | solution.py:438
  12.3 16.5 %collective-permute-start.2 = (f32[8,64,256]{2,1,0:T(8,128)}, f32[8,64,256]{2,1,0:T(8,128)S(1)}, u32[]{:S(2)}, u32[]{:S(2)}) collective-permute-start(f32[8,64,256]{2,1,0:T(8,128)} %get-tuple-element.46), channel_id=1, source_target_pairs={{0,24},{2,26},{4,28},{6,30},{8,16},{10,18},{12,20},{14,22},{16,8},... | collective-permute-start | bytes 1572872 | tf_op jit(solution)/shard_map/ppermute | solution.py:438
  24.2 29.6 %all-to-all-start = ((bf16[64,32,256]{2,1,0:T(8,128)(2,1)}), bf16[64,32,256]{2,1,0:T(8,128)(2,1)S(1)}, u32[]{:S(2)}, u32[]{:S(2)}) async-start(bf16[64,32,256]{2,1,0:T(8,128)(2,1)} %get-tuple-element.56), calls=%async_computation | async-start | bytes 2097152 | tf_op jit(solution)/shard_map/all_to_all | solution.py:442
  28.9 0.8 copy-start.2
  28.9 1.0 copy-start
  29.9 0.9 copy-start.1
  36.6 14.9 %collective-permute-start.5 = (f32[4,96,256]{2,1,0:T(8,128)}, f32[4,96,256]{2,1,0:T(8,128)S(1)}, u32[]{:S(2)}, u32[]{:S(2)}) collective-permute-start(f32[4,96,256]{2,1,0:T(8,128)} %get-tuple-element.55), channel_id=1, source_target_pairs={{0,2},{2,0},{4,6},{6,4},{8,10},{10,8},{12,14},{14,12},{16,18},{18,... | collective-permute-start | bytes 1179656 | tf_op jit(solution)/shard_map/ppermute | solution.py:444
  37.6 15.0 %collective-permute-start.3 = (f32[4,96,256]{2,1,0:T(8,128)}, f32[4,96,256]{2,1,0:T(8,128)S(1)}, u32[]{:S(2)}, u32[]{:S(2)}) collective-permute-start(f32[4,96,256]{2,1,0:T(8,128)} %get-tuple-element.51), channel_id=1, source_target_pairs={{0,32},{2,34},{4,36},{6,38},{8,40},{10,42},{12,44},{14,46},{16,48}... | collective-permute-start | bytes 1179656 | tf_op jit(solution)/shard_map/ppermute | solution.py:444
  38.9 11.6 %collective-permute-start.4 = (f32[4,64,256]{2,1,0:T(8,128)}, f32[4,64,256]{2,1,0:T(8,128)S(1)}, u32[]{:S(2)}, u32[]{:S(2)}) collective-permute-start(f32[4,64,256]{2,1,0:T(8,128)} %get-tuple-element.53), channel_id=1, source_target_pairs={{0,8},{2,10},{4,12},{6,14},{8,0},{10,2},{12,4},{14,6},{16,24},{18,... | collective-permute-start | bytes 786440 | tf_op jit(solution)/shard_map/ppermute | solution.py:444
  53.7 19.9 %copy-start.4 = (f32[32,256]{1,0:T(8,128)S(1)}, f32[32,256]{1,0:T(8,128)}, u32[]{:S(2)}) copy-start(f32[32,256]{1,0:T(8,128)} %get-tuple-element.63) | copy-start | bytes 98308
  53.7 7.3 %collective-permute-start.7 = (f32[2,96,256]{2,1,0:T(8,128)S(1)}, f32[2,96,256]{2,1,0:T(8,128)S(1)}, u32[]{:S(2)}, u32[]{:S(2)}) collective-permute-start(f32[2,96,256]{2,1,0:T(8,128)S(1)} %constant_dynamic-slice_fusion.5), channel_id=1, source_target_pairs={{0,96},{2,98},{4,100},{6,102},{8,104},{10,106},{12,108},{14,110},{... | collective-permute-start | bytes 589832 | tf_op jit(solution)/shard_map/ppermute | solution.py:463
  54.3 8.8 %collective-permute-start.6 = (f32[2,160,256]{2,1,0:T(8,128)S(1)}, f32[2,160,256]{2,1,0:T(8,128)S(1)}, u32[]{:S(2)}, u32[]{:S(2)}) collective-permute-start(f32[2,160,256]{2,1,0:T(8,128)S(1)} %fusion), channel_id=1, source_target_pairs={{0,6},{2,4},{4,2},{6,0},{8,14},{10,12},{12,10},{14,8},{16,22},{18,... | collective-permute-start | bytes 983048 | tf_op jit(solution)/shard_map/ppermute | solution.py:463
  63.2 3.5 %collective-permute-start.9 = (f32[1,96,256]{2,1,0:T(8,128)S(1)}, f32[1,96,256]{2,1,0:T(8,128)S(1)}, u32[]{:S(2)}, u32[]{:S(2)}) collective-permute-start(f32[1,96,256]{2,1,0:T(8,128)S(1)} %constant_dynamic-slice_fusion.3), channel_id=1, source_target_pairs={{0,32},{2,34},{4,36},{6,38},{8,40},{10,42},{12,44},{14,46},{16,48}... | collective-permute-start | bytes 294920 | tf_op jit(solution)/shard_map/ppermute | solution.py:463
  64.1 9.4 %collective-permute-start.11 = (bf16[64,16,256]{2,1,0:T(8,128)(2,1)S(1)}, bf16[64,16,256]{2,1,0:T(8,128)(2,1)S(1)}, u32[]{:S(2)}, u32[]{:S(2)}) collective-permute-start(bf16[64,16,256]{2,1,0:T(8,128)(2,1)S(1)} %get-tuple-element.70), channel_id=1, source_target_pairs={{0,1},{1,0},{2,3},{3,2},{4,5},{5,4},{6,7},{7,6},{8,9},{9,8},{10,11... | collective-permute-start | bytes 1572872 | tf_op jit(solution)/shard_map/ppermute | solution.py:459
  66.7 5.8 %collective-permute-start.8 = (f32[1,160,256]{2,1,0:T(8,128)S(1)}, f32[1,160,256]{2,1,0:T(8,128)S(1)}, u32[]{:S(2)}, u32[]{:S(2)}) collective-permute-start(f32[1,160,256]{2,1,0:T(8,128)S(1)} %constant_dynamic-slice_fusion.4), channel_id=1, source_target_pairs={{0,2},{2,0},{4,6},{6,4},{8,10},{10,8},{12,14},{14,12},{16,18},{18,... | collective-permute-start | bytes 491528 | tf_op jit(solution)/shard_map/ppermute | solution.py:463
  72.5 2.1 %collective-permute-start.10 = (f32[256,256]{1,0:T(8,128)S(1)}, f32[256,256]{1,0:T(8,128)S(1)}, u32[]{:S(2)}, u32[]{:S(2)}) collective-permute-start(f32[256,256]{1,0:T(8,128)S(1)} %pad_maximum_fusion), channel_id=1, source_target_pairs={{0,1},{1,0},{2,3},{3,2},{4,5},{5,4},{6,7},{7,6},{8,9},{9,8},{10,11... | collective-permute-start | bytes 786440 | tf_op jit(solution)/shard_map/ppermute | solution.py:464
  102.3 44.5 %copy-start.3 = (f32[16,256]{1,0:T(8,128)}, f32[16,256]{1,0:T(8,128)S(1)}, u32[]{:S(2)}) copy-start(f32[16,256]{1,0:T(8,128)S(1)} %add.111) | copy-start | bytes 49156
  124.0 5.6 %collective-permute-start.12 = (f32[64,16,256]{2,1,0:T(8,128)S(1)}, f32[64,16,256]{2,1,0:T(8,128)S(1)}, u32[]{:S(2)}, u32[]{:S(2)}) collective-permute-start(f32[64,16,256]{2,1,0:T(8,128)S(1)} %all_to_all.16), channel_id=1, source_target_pairs={{0,1},{1,0},{2,3},{3,2},{4,5},{5,4},{6,7},{7,6},{8,9},{9,8},{10,11... | collective-permute-start | bytes 3145736 | tf_op jit(solution)/shard_map/ppermute | solution.py:473

commit v4 on v3

--- a/solution.py
+++ b/solution.py
@@ -151,20 +151,21 @@
 NEAR = 0.0025
 
 
-def tail_kernel(where_ref, mine_ref, other_ref, basis_ref, factor_ref, gram_ref, held, work, upper, first_upper):
+def gram_kernel(value, out):
+    out[...] = gram_of(split3(value[...]))
+
+
+def tail_kernel(where_ref, mine_ref, other_ref, mine_gram, basis_ref, factor_ref, gram_ref, held, work, upper, first_upper):
     n = work.shape[0]
     rows = basis_ref.shape[0]
     part = mine_ref.shape[0]
     total = float(2 * part)
     scale = total ** 0.5
-    lane = where_ref[0]
-    held[pl.ds(pl.multiple_of(lane * part, part), part), :] = mine_ref[...]
-    held[pl.ds(pl.multiple_of((1 - lane) * part, part), part), :] = other_ref[...]
     row = lax.broadcasted_iota(jnp.int32, (n, n), 0)
     col = lax.broadcasted_iota(jnp.int32, (n, n), 1)
     identity = jnp.where(row == col, 1.0, 0.0)
-    at = pl.multiple_of(where_ref[1], 16)
-    gram1 = gram_of(split3(held[...]))
+    at = pl.multiple_of(where_ref[0], 16)
+    gram1 = mine_gram[...] + gram_of(split3(other_ref[...]))
     gram_ref[...] = gram1 / total
     work[...] = gram1
 
@@ -175,9 +176,10 @@
         def after_first():
             first_upper[...] = upper[...]
             inverse = jnp.where(col <= row, work[...], 0.0)
-            first = times_transposed(split3(held[...]), inverse)
+            first = times_transposed(split3(mine_ref[...]), inverse)
             held[...] = first
             gram2 = gram_of(split3(first))
+            gram2 = gram2 + gram_of(split3(times_transposed(split3(other_ref[...]), inverse)))
             work[...] = gram2
             error = gram2 - identity
             return jnp.where(jnp.sum(error * error) <= NEAR, 0, 1)
@@ -208,7 +210,19 @@
         factor_ref[...] = jnp.dot(upper[...], first_upper[...], precision=HIGH, preferred_element_type=F32) / scale
 
 
-def tail(mine, other, where, rows):
+def half_gram(mine):
+    n = mine.shape[1]
+    vmem = pl.BlockSpec(memory_space=pltpu.VMEM)
+    return pl.pallas_call(
+        gram_kernel,
+        out_shape=jax.ShapeDtypeStruct((n, n), F32),
+        in_specs=[vmem],
+        out_specs=vmem,
+        compiler_params=pltpu.CompilerParams(vmem_limit_bytes=16 * 1024 * 1024),
+    )(mine)
+
+
+def tail(mine, other, mine_gram, where, rows):
     part, n = mine.shape
     vmem = pl.BlockSpec(memory_space=pltpu.VMEM)
     return pl.pallas_call(
@@ -218,16 +232,16 @@
             jax.ShapeDtypeStruct((n, n), F32),
             jax.ShapeDtypeStruct((n, n), F32),
         ),
-        in_specs=[pl.BlockSpec(memory_space=pltpu.SMEM), vmem, vmem],
+        in_specs=[pl.BlockSpec(memory_space=pltpu.SMEM), vmem, vmem, vmem],
         out_specs=(vmem, vmem, vmem),
         scratch_shapes=[
-            pltpu.VMEM((2 * part, n), F32),
+            pltpu.VMEM((part, n), F32),
             pltpu.VMEM((n, n), F32),
             pltpu.VMEM((n, n), F32),
             pltpu.VMEM((n, n), F32),
         ],
         compiler_params=pltpu.CompilerParams(vmem_limit_bytes=24 * 1024 * 1024),
-    )(where, mine, other)
+    )(where, mine, other, mine_gram)
 
 
 SIDE = 4
@@ -464,7 +478,7 @@
     away = lax.ppermute(jnp.concatenate([keep[0] for keep in keeps], axis=0), "pw", SWAP)
     both = couple(keeps, away, own_rows, other_rows)
     own_diagonal = lax.dynamic_slice_in_dim(diagonal, lane * half, half, 0)
-    where = jnp.stack([lane, lane * (cells * half) + place * half]).astype(jnp.int32)
+    where = (place * half).astype(jnp.int32).reshape(1)
     both, own_diagonal, where = lax.optimization_barrier((both, own_diagonal, where))
     arrived = lax.all_to_all(both, "col", split_axis=0, concat_axis=0, tiled=True)
     sketch = jnp.sum(arrived, axis=0) + own_diagonal
@@ -472,7 +486,8 @@
     mine = lax.all_to_all(copies, "col", split_axis=0, concat_axis=0, tiled=True)
     other = lax.ppermute(mine, "pw", SWAP)
     rank = sketch.shape[1]
-    basis, factor, gram = tail(mine.reshape(cells * half, rank), other.reshape(cells * half, rank), where, half)
+    mine, other = mine.reshape(cells * half, rank), other.reshape(cells * half, rank)
+    basis, factor, gram = tail(mine, other, half_gram(mine), where, half)
     return (sketch, basis, factor, gram)
 
 

time: 147 us -> 146 us (level)
    pallas_call x1, Pallas kernels: 17.2 us -> 15.7 us  [tail(): pl.pallas_call(tail_kernel, out_shape=(jax.ShapeDtypeStruct((rows, n), F3...]
where the time goes in v4:
time: 146 us; the launch traced here: 145 us
  blocking collectives  48.2 us (33%)
  Pallas kernels  35.2 us (24%)
  starting transfers between devices  28.1 us (19%)
  waiting for transfers between devices  26 us (18%)
  other arithmetic  3.92 us (3%)
  local copies, waits for them, and re-layouts  3.07 us (2%)
    all_to_all x1, blocking collectives, shards(): lax.all_to_all(both, 'col', split_axis=0, concat_axis=0, tiled=True)  26.6 us
    all_to_all x1, blocking collectives, shards(): lax.all_to_all(copies, 'col', split_axis=0, concat_axis=0, tiled=True)  21.6 us
    pallas_call x1, Pallas kernels, tail(): pl.pallas_call(tail_kernel, out_shape=(jax.ShapeDtypeStruct((rows, n), F3...  15.7 us
    ppermute x4, waiting for transfers between devices, shards(): lax.ppermute(gives[part], 'col', neighbours(order[1], size > 1))  12.5 us
    pallas_call x2, Pallas kernels, image_call(): pl.pallas_call(send_kernel if came is None else keep_kernel, grid_spec=pl...  10.8 us
    ppermute x3, waiting for transfers between devices, shards(): lax.ppermute(give, 'col', neighbours(order[0], False))  10.4 us
    ppermute x3, starting transfers between devices, shards(): lax.ppermute(give, 'col', neighbours(order[0], True))  9.8 us
    pallas_call x1, Pallas kernels, rows_call(): pl.pallas_call(rows_kernel, grid=(steps,), in_specs=[whole(1, count), who...  6.89 us
  transfers between devices with their start and end apart: 14, of which 7 were waited for; matrix products, arithmetic and copies ran while one was open for 3% of the time, Pallas kernels for 9%

profile of v4, /device:TPU:1, one launch (start us, length us, event | category | flops | bytes accessed | tf_op | source)
XLA Modules:
  0.0 145.3 jit_solution(6058612248328869828)
XLA Ops:
  0.8 0.6 add_subtract_fusion.half
  1.3 0.0 copy-start.5
  1.3 4.9 %shard_map.84 = (f32[8,96,256]{2,1,0:T(8,128)}, f32[8,96,256]{2,1,0:T(8,128)}, f32[8,64,256]{2,1,0:T(8,128)}) custom-call(s32[3]{0:T(128)} %add_subtract_fusion.half, bf16[896,256]{1,0:T(8,128)(2,1)} %test.5, bf16[2048,896]{1,0:T(8,128)(2,1)} %x_short.5, bf16[2048,896]{1,0:T(8,128)(2,1)} %x_short.5, bf16[2048,896]{1,0:T(8,128)(2,1)} %y_short.5, ...), custom_call_target="tpu_custom_call" | custom-call | tf_op jit(solution)/shard_map/pallas_call | solution.py:328
  6.3 3.3 %collective-permute-start = (f32[8,96,256]{2,1,0:T(8,128)}, f32[8,96,256]{2,1,0:T(8,128)S(1)}, u32[]{:S(2)}, u32[]{:S(2)}) collective-permute-start(f32[8,96,256]{2,1,0:T(8,128)} %get-tuple-element.44), channel_id=1, source_target_pairs={{0,96},{2,98},{4,100},{6,102},{8,104},{10,106},{12,108},{14,110},{... | collective-permute-start | bytes 2359304 | tf_op jit(solution)/shard_map/ppermute | solution.py:452
  9.6 2.7 %collective-permute-start.1 = (f32[8,96,256]{2,1,0:T(8,128)}, f32[8,96,256]{2,1,0:T(8,128)S(1)}, u32[]{:S(2)}, u32[]{:S(2)}) collective-permute-start(f32[8,96,256]{2,1,0:T(8,128)} %get-tuple-element.45), channel_id=1, source_target_pairs={{0,6},{2,4},{4,2},{6,0},{8,14},{10,12},{12,10},{14,8},{16,22},{18,... | collective-permute-start | bytes 2359304 | tf_op jit(solution)/shard_map/ppermute | solution.py:452
  12.3 3.7 %collective-permute-start.2 = (f32[8,64,256]{2,1,0:T(8,128)}, f32[8,64,256]{2,1,0:T(8,128)S(1)}, u32[]{:S(2)}, u32[]{:S(2)}) collective-permute-start(f32[8,64,256]{2,1,0:T(8,128)} %get-tuple-element.46), channel_id=1, source_target_pairs={{0,24},{2,26},{4,28},{6,30},{8,16},{10,18},{12,20},{14,22},{16,8},... | collective-permute-start | bytes 1572872 | tf_op jit(solution)/shard_map/ppermute | solution.py:452
  16.1 0.0 copy-done.5
  16.1 0.6 reshape.21.energy_row
  16.7 6.9 %shard_map.85 = (bf16[64,32,256]{2,1,0:T(8,128)(2,1)}, f32[32,256]{1,0:T(8,128)}) custom-call(s32[1,32]{1,0:T(1,128)} %picks_row, f32[1,896]{1,0:T(1,128)} %reshape.21.energy_row, bf16[896,256]{1,0:T(8,128)(2,1)} %test.5, bf16[2048,896]{1,0:T(8,128)(2,1)} %x_short.5, bf16[2048,896]{1,0:T(8,128)(2,1)} %x_short.5, bf16[2048,896]{1,0:T(8,128)(2,1)} %y_short.5, ...), custom_call_target="tpu_custom_call" | custom-call | tf_op jit(solution)/shard_map/pallas_call | solution.py:391
  23.6 0.6 concatenate.10.half
  24.2 4.7 %all-to-all-start = ((bf16[64,32,256]{2,1,0:T(8,128)(2,1)}), bf16[64,32,256]{2,1,0:T(8,128)(2,1)S(1)}, u32[]{:S(2)}, u32[]{:S(2)}) async-start(bf16[64,32,256]{2,1,0:T(8,128)(2,1)} %get-tuple-element.56), calls=%async_computation | async-start | bytes 2097152 | tf_op jit(solution)/shard_map/all_to_all | solution.py:456
  28.8 0.0 collective-permute-done.2.refs_2_
  28.9 0.0 copy-start.2
  28.9 0.0 collective-permute-done.refs_0_
  28.9 0.0 copy-start
  28.9 0.4 collective-permute-done.1.refs_1_
  29.3 0.4 copy-done.2
  29.6 0.3 copy-done
  29.9 0.0 copy-start.1
  29.9 0.9 copy-done.1
  30.8 5.8 %shard_map.86 = (f32[4,96,256]{2,1,0:T(8,128)}, f32[4,96,256]{2,1,0:T(8,128)}, f32[4,64,256]{2,1,0:T(8,128)}, f32[4,96,256]{2,1,0:T(8,128)}, f32[4,96,256]{2,1,0:T(8,128)}, /*index=5*/f32[4,64,256]{2,1,0:T(8,128)}) custom-call(s32[6]{0:T(128)} %concatenate.10.half, bf16[896,256]{1,0:T(8,128)(2,1)} %test.5, bf16[2048,896]{1,0:T(8,128)(2,1)} %x_short.5, ...), custom_call_target="tpu_custom_call" | custom-call | tf_op jit(solution)/shard_map/pallas_call | solution.py:328
  36.6 1.0 collective-permute-start.5
  37.6 1.3 collective-permute-start.3
  38.9 1.2 collective-permute-start.4
  40.1 10.4 %collective-permute-done.4 = f32[4,64,256]{2,1,0:T(8,128)S(1)} collective-permute-done((f32[4,64,256]{2,1,0:T(8,128)}, f32[4,64,256]{2,1,0:T(8,128)S(1)}, u32[]{:S(2)}, u32[]{:S(2)}) %collective-permute-start.4) | collective-permute-done | bytes 262176 | tf_op jit(solution)/shard_map/ppermute | solution.py:458
  50.6 1.0 add.91
  51.5 0.0 collective-permute-done.5
  51.5 1.0 add.94
  52.6 0.0 collective-permute-done.3
  52.6 1.0 add.90
  53.7 0.0 copy-start.4
  53.7 0.0 all-to-all-done
  53.7 0.5 collective-permute-start.7
  54.3 2.0 %collective-permute-start.6 = (f32[2,160,256]{2,1,0:T(8,128)S(1)}, f32[2,160,256]{2,1,0:T(8,128)S(1)}, u32[]{:S(2)}, u32[]{:S(2)}) collective-permute-start(f32[2,160,256]{2,1,0:T(8,128)S(1)} %fusion), channel_id=1, source_target_pairs={{0,6},{2,4},{4,2},{6,0},{8,14},{10,12},{12,10},{14,8},{16,22},{18,... | collective-permute-start | bytes 983048 | tf_op jit(solution)/shard_map/ppermute | solution.py:477
  56.3 4.7 %collective-permute-done.7 = f32[2,96,256]{2,1,0:T(8,128)S(1)} collective-permute-done((f32[2,96,256]{2,1,0:T(8,128)S(1)}, f32[2,96,256]{2,1,0:T(8,128)S(1)}, u32[]{:S(2)}, u32[]{:S(2)}) %collective-permute-start.7) | collective-permute-done | bytes 196640 | tf_op jit(solution)/shard_map/ppermute | solution.py:477
  61.1 2.0 %collective-permute-done.6 = f32[2,160,256]{2,1,0:T(8,128)S(1)} collective-permute-done((f32[2,160,256]{2,1,0:T(8,128)S(1)}, f32[2,160,256]{2,1,0:T(8,128)S(1)}, u32[]{:S(2)}, u32[]{:S(2)}) %collective-permute-start.6) | collective-permute-done | bytes 327712 | tf_op jit(solution)/shard_map/ppermute | solution.py:477
  63.2 0.8 collective-permute-start.9
  64.0 0.1 constant_dynamic-slice_fusion.1
  64.1 2.6 %collective-permute-start.11 = (bf16[64,16,256]{2,1,0:T(8,128)(2,1)S(1)}, bf16[64,16,256]{2,1,0:T(8,128)(2,1)S(1)}, u32[]{:S(2)}, u32[]{:S(2)}) collective-permute-start(bf16[64,16,256]{2,1,0:T(8,128)(2,1)S(1)} %get-tuple-element.70), channel_id=1, source_target_pairs={{0,1},{1,0},{2,3},{3,2},{4,5},{5,4},{6,7},{7,6},{8,9},{9,8},{10,11... | collective-permute-start | bytes 1572872 | tf_op jit(solution)/shard_map/ppermute | solution.py:473
  66.7 0.0 collective-permute-start.8
  66.7 0.0 collective-permute-done.9
  66.7 5.7 %collective-permute-done.8 = f32[1,160,256]{2,1,0:T(8,128)S(1)} collective-permute-done((f32[1,160,256]{2,1,0:T(8,128)S(1)}, f32[1,160,256]{2,1,0:T(8,128)S(1)}, u32[]{:S(2)}, u32[]{:S(2)}) %collective-permute-start.8) | collective-permute-done | bytes 163872 | tf_op jit(solution)/shard_map/ppermute | solution.py:477
  72.5 1.0 collective-permute-start.10
  73.4 0.0 copy-done.4
  73.4 0.0 collective-permute-done.11.other_rows
  73.4 1.2 collective-permute-done.10.away
  74.6 1.0 shard_map.87
  75.6 26.6 %all_to_all.15 = f32[64,16,256]{2,1,0:T(8,128)S(1)} all-to-all(f32[64,16,256]{2,1,0:T(8,128)S(1)} %shard_map.87), channel_id=1, replica_groups=mesh['col'=64,'pw'=2] {'col'}, dimensions={0} | all-to-all | bytes 2097152 | tf_op jit(solution)/shard_map/all_to_all | solution.py:483
  102.1 0.1 reduce_sum.9
  102.3 0.0 copy-start.3
  102.3 0.1 broadcast_in_dim.2
  102.4 21.6 %all_to_all.16 = f32[64,16,256]{2,1,0:T(8,128)S(1)} all-to-all(f32[64,16,256]{2,1,0:T(8,128)S(1)} %broadcast_in_dim.2), channel_id=1, replica_groups=mesh['col'=64,'pw'=2] {'col'}, dimensions={0} | all-to-all | bytes 2097152 | tf_op jit(solution)/shard_map/all_to_all | solution.py:486
  124.0 3.3 %collective-permute-start.12 = (f32[64,16,256]{2,1,0:T(8,128)S(1)}, f32[64,16,256]{2,1,0:T(8,128)S(1)}, u32[]{:S(2)}, u32[]{:S(2)}) collective-permute-start(f32[64,16,256]{2,1,0:T(8,128)S(1)} %all_to_all.16), channel_id=1, source_target_pairs={{0,1},{1,0},{2,3},{3,2},{4,5},{5,4},{6,7},{7,6},{8,9},{9,8},{10,11... | collective-permute-start | bytes 3145736 | tf_op jit(solution)/shard_map/ppermute | solution.py:487
  127.3 0.8 shard_map.88.mine_gram
  128.1 1.5 %collective-permute-done.12 = f32[64,16,256]{2,1,0:T(8,128)S(1)} collective-permute-done((f32[64,16,256]{2,1,0:T(8,128)S(1)}, f32[64,16,256]{2,1,0:T(8,128)S(1)}, u32[]{:S(2)}, u32[]{:S(2)}) %collective-permute-start.12) | collective-permute-done | bytes 1048608 | tf_op jit(solution)/shard_map/ppermute | solution.py:487
  129.6 15.7 %shard_map.89 = (f32[16,256]{1,0:T(8,128)}, f32[256,256]{1,0:T(8,128)}, f32[256,256]{1,0:T(8,128)}) custom-call(s32[1]{0:T(128)} %bitcast.8.where_ref, f32[1024,256]{1,0:T(8,128)S(1)} %bitcast.12, f32[1024,256]{1,0:T(8,128)S(1)} %bitcast.14, f32[256,256]{1,0:T(8,128)S(1)} %shard_map.88.mine_gram), custom_call_target="tpu_custom_call" | custom-call | tf_op jit(solution)/shard_map/pallas_call | solution.py:228
  145.3 0.0 copy-done.3
  (11 shorter events, 0.2 us)
Async XLA Ops:
  1.3 14.7 %copy-start.5 = (f32[896]{0:T(1024)S(1)}, f32[896]{0:T(1024)}, u32[]{:S(2)}) copy-start(f32[896]{0:T(1024)} %param.8) | copy-start | bytes 10756
  6.3 22.6 %collective-permute-start = (f32[8,96,256]{2,1,0:T(8,128)}, f32[8,96,256]{2,1,0:T(8,128)S(1)}, u32[]{:S(2)}, u32[]{:S(2)}) collective-permute-start(f32[8,96,256]{2,1,0:T(8,128)} %get-tuple-element.44), channel_id=1, source_target_pairs={{0,96},{2,98},{4,100},{6,102},{8,104},{10,106},{12,108},{14,110},{... | collective-permute-start | bytes 2359304 | tf_op jit(solution)/shard_map/ppermute | solution.py:452
  9.6 19.7 %collective-permute-start.1 = (f32[8,96,256]{2,1,0:T(8,128)}, f32[8,96,256]{2,1,0:T(8,128)S(1)}, u32[]{:S(2)}, u32[]{:S(2)}) collective-permute-start(f32[8,96,256]{2,1,0:T(8,128)} %get-tuple-element.45), channel_id=1, source_target_pairs={{0,6},{2,4},{4,2},{6,0},{8,14},{10,12},{12,10},{14,8},{16,22},{18,... | collective-permute-start | bytes 2359304 | tf_op jit(solution)/shard_map/ppermute | solution.py:452
  12.3 16.5 %collective-permute-start.2 = (f32[8,64,256]{2,1,0:T(8,128)}, f32[8,64,256]{2,1,0:T(8,128)S(1)}, u32[]{:S(2)}, u32[]{:S(2)}) collective-permute-start(f32[8,64,256]{2,1,0:T(8,128)} %get-tuple-element.46), channel_id=1, source_target_pairs={{0,24},{2,26},{4,28},{6,30},{8,16},{10,18},{12,20},{14,22},{16,8},... | collective-permute-start | bytes 1572872 | tf_op jit(solution)/shard_map/ppermute | solution.py:452
  24.2 29.6 %all-to-all-start = ((bf16[64,32,256]{2,1,0:T(8,128)(2,1)}), bf16[64,32,256]{2,1,0:T(8,128)(2,1)S(1)}, u32[]{:S(2)}, u32[]{:S(2)}) async-start(bf16[64,32,256]{2,1,0:T(8,128)(2,1)} %get-tuple-element.56), calls=%async_computation | async-start | bytes 2097152 | tf_op jit(solution)/shard_map/all_to_all | solution.py:456
  28.9 0.8 copy-start.2
  28.9 1.0 copy-start
  29.9 0.9 copy-start.1
  36.6 14.9 %collective-permute-start.5 = (f32[4,96,256]{2,1,0:T(8,128)}, f32[4,96,256]{2,1,0:T(8,128)S(1)}, u32[]{:S(2)}, u32[]{:S(2)}) collective-permute-start(f32[4,96,256]{2,1,0:T(8,128)} %get-tuple-element.55), channel_id=1, source_target_pairs={{0,2},{2,0},{4,6},{6,4},{8,10},{10,8},{12,14},{14,12},{16,18},{18,... | collective-permute-start | bytes 1179656 | tf_op jit(solution)/shard_map/ppermute | solution.py:458
  37.6 15.0 %collective-permute-start.3 = (f32[4,96,256]{2,1,0:T(8,128)}, f32[4,96,256]{2,1,0:T(8,128)S(1)}, u32[]{:S(2)}, u32[]{:S(2)}) collective-permute-start(f32[4,96,256]{2,1,0:T(8,128)} %get-tuple-element.51), channel_id=1, source_target_pairs={{0,32},{2,34},{4,36},{6,38},{8,40},{10,42},{12,44},{14,46},{16,48}... | collective-permute-start | bytes 1179656 | tf_op jit(solution)/shard_map/ppermute | solution.py:458
  38.9 11.6 %collective-permute-start.4 = (f32[4,64,256]{2,1,0:T(8,128)}, f32[4,64,256]{2,1,0:T(8,128)S(1)}, u32[]{:S(2)}, u32[]{:S(2)}) collective-permute-start(f32[4,64,256]{2,1,0:T(8,128)} %get-tuple-element.53), channel_id=1, source_target_pairs={{0,8},{2,10},{4,12},{6,14},{8,0},{10,2},{12,4},{14,6},{16,24},{18,... | collective-permute-start | bytes 786440 | tf_op jit(solution)/shard_map/ppermute | solution.py:458
  53.7 19.8 %copy-start.4 = (f32[32,256]{1,0:T(8,128)S(1)}, f32[32,256]{1,0:T(8,128)}, u32[]{:S(2)}) copy-start(f32[32,256]{1,0:T(8,128)} %get-tuple-element.63) | copy-start | bytes 98308
  53.7 7.3 %collective-permute-start.7 = (f32[2,96,256]{2,1,0:T(8,128)S(1)}, f32[2,96,256]{2,1,0:T(8,128)S(1)}, u32[]{:S(2)}, u32[]{:S(2)}) collective-permute-start(f32[2,96,256]{2,1,0:T(8,128)S(1)} %constant_dynamic-slice_fusion.5), channel_id=1, source_target_pairs={{0,96},{2,98},{4,100},{6,102},{8,104},{10,106},{12,108},{14,110},{... | collective-permute-start | bytes 589832 | tf_op jit(solution)/shard_map/ppermute | solution.py:477
  54.3 8.8 %collective-permute-start.6 = (f32[2,160,256]{2,1,0:T(8,128)S(1)}, f32[2,160,256]{2,1,0:T(8,128)S(1)}, u32[]{:S(2)}, u32[]{:S(2)}) collective-permute-start(f32[2,160,256]{2,1,0:T(8,128)S(1)} %fusion), channel_id=1, source_target_pairs={{0,6},{2,4},{4,2},{6,0},{8,14},{10,12},{12,10},{14,8},{16,22},{18,... | collective-permute-start | bytes 983048 | tf_op jit(solution)/shard_map/ppermute | solution.py:477
  63.2 3.5 %collective-permute-start.9 = (f32[1,96,256]{2,1,0:T(8,128)S(1)}, f32[1,96,256]{2,1,0:T(8,128)S(1)}, u32[]{:S(2)}, u32[]{:S(2)}) collective-permute-start(f32[1,96,256]{2,1,0:T(8,128)S(1)} %constant_dynamic-slice_fusion.3), channel_id=1, source_target_pairs={{0,32},{2,34},{4,36},{6,38},{8,40},{10,42},{12,44},{14,46},{16,48}... | collective-permute-start | bytes 294920 | tf_op jit(solution)/shard_map/ppermute | solution.py:477
  64.1 9.4 %collective-permute-start.11 = (bf16[64,16,256]{2,1,0:T(8,128)(2,1)S(1)}, bf16[64,16,256]{2,1,0:T(8,128)(2,1)S(1)}, u32[]{:S(2)}, u32[]{:S(2)}) collective-permute-start(bf16[64,16,256]{2,1,0:T(8,128)(2,1)S(1)} %get-tuple-element.70), channel_id=1, source_target_pairs={{0,1},{1,0},{2,3},{3,2},{4,5},{5,4},{6,7},{7,6},{8,9},{9,8},{10,11... | collective-permute-start | bytes 1572872 | tf_op jit(solution)/shard_map/ppermute | solution.py:473
  66.7 5.8 %collective-permute-start.8 = (f32[1,160,256]{2,1,0:T(8,128)S(1)}, f32[1,160,256]{2,1,0:T(8,128)S(1)}, u32[]{:S(2)}, u32[]{:S(2)}) collective-permute-start(f32[1,160,256]{2,1,0:T(8,128)S(1)} %constant_dynamic-slice_fusion.4), channel_id=1, source_target_pairs={{0,2},{2,0},{4,6},{6,4},{8,10},{10,8},{12,14},{14,12},{16,18},{18,... | collective-permute-start | bytes 491528 | tf_op jit(solution)/shard_map/ppermute | solution.py:477
  72.5 2.1 %collective-permute-start.10 = (f32[256,256]{1,0:T(8,128)S(1)}, f32[256,256]{1,0:T(8,128)S(1)}, u32[]{:S(2)}, u32[]{:S(2)}) collective-permute-start(f32[256,256]{1,0:T(8,128)S(1)} %pad_maximum_fusion), channel_id=1, source_target_pairs={{0,1},{1,0},{2,3},{3,2},{4,5},{5,4},{6,7},{7,6},{8,9},{9,8},{10,11... | collective-permute-start | bytes 786440 | tf_op jit(solution)/shard_map/ppermute | solution.py:478
  102.3 43.1 %copy-start.3 = (f32[16,256]{1,0:T(8,128)}, f32[16,256]{1,0:T(8,128)S(1)}, u32[]{:S(2)}) copy-start(f32[16,256]{1,0:T(8,128)S(1)} %add.107) | copy-start | bytes 49156
  124.0 5.6 %collective-permute-start.12 = (f32[64,16,256]{2,1,0:T(8,128)S(1)}, f32[64,16,256]{2,1,0:T(8,128)S(1)}, u32[]{:S(2)}, u32[]{:S(2)}) collective-permute-start(f32[64,16,256]{2,1,0:T(8,128)S(1)} %all_to_all.16), channel_id=1, source_target_pairs={{0,1},{1,0},{2,3},{3,2},{4,5},{5,4},{6,7},{7,6},{8,9},{9,8},{10,11... | collective-permute-start | bytes 3145736 | tf_op jit(solution)/shard_map/ppermute | solution.py:487

commit v5 on v4

--- a/solution.py
+++ b/solution.py
@@ -404,7 +404,7 @@
             pltpu.VMEM((width, count), jnp.bfloat16),
             pltpu.VMEM((3, slices, count, together), F32),
         ],
-        compiler_params=pltpu.CompilerParams(vmem_limit_bytes=56 * 1024 * 1024),
+        compiler_params=pltpu.CompilerParams(vmem_limit_bytes=24 * 1024 * 1024),
     )(picks, energies.reshape(1, width), test, exchange, exchange, direct, direct)
 
 

time: 146 us -> 145 us (level)
  local copies, waits for them, and re-layouts: 3.07 us -> 6.69 us
  Pallas kernels: 35.2 us -> 31.9 us
    unnamed x12 -> x16, local copies, waits for them, and re-layouts: 1.58 us -> 5.78 us
    pallas_call x1, Pallas kernels: 6.89 us -> 3.64 us  [rows_call(): pl.pallas_call(rows_kernel, grid=(steps,), in_specs=[whole(1, count), who...]
  transfers between devices with their start and end apart: 14 -> 14, of which waited for: 7 -> 8; matrix products, arithmetic and copies ran while one was open for 3% -> 3% of each run, Pallas kernels for 9% -> 7%
where the time goes in v5:
time: 145 us
  blocking collectives  47.5 us (33%)
  Pallas kernels  31.9 us (22%)
  starting transfers between devices  27.9 us (19%)
  waiting for transfers between devices  26 us (18%)
  local copies, waits for them, and re-layouts  6.69 us (5%)
  other arithmetic  3.92 us (3%)
    all_to_all x1, blocking collectives, shards(): lax.all_to_all(both, 'col', split_axis=0, concat_axis=0, tiled=True)  25.9 us
    all_to_all x1, blocking collectives, shards(): lax.all_to_all(copies, 'col', split_axis=0, concat_axis=0, tiled=True)  21.6 us
    pallas_call x1, Pallas kernels, tail(): pl.pallas_call(tail_kernel, out_shape=(jax.ShapeDtypeStruct((rows, n), F3...  15.7 us
    ppermute x4, waiting for transfers between devices, shards(): lax.ppermute(gives[part], 'col', neighbours(order[1], size > 1))  12.7 us
    pallas_call x2, Pallas kernels, image_call(): pl.pallas_call(send_kernel if came is None else keep_kernel, grid_spec=pl...  10.7 us
    ppermute x3, waiting for transfers between devices, shards(): lax.ppermute(give, 'col', neighbours(order[0], False))  10.6 us
    ppermute x3, starting transfers between devices, shards(): lax.ppermute(give, 'col', neighbours(order[0], True))  9.8 us
    unnamed x16, local copies, waits for them, and re-layouts  5.78 us
  transfers between devices with their start and end apart: 14, of which 8 were waited for; matrix products, arithmetic and copies ran while one was open for 3% of the time, Pallas kernels for 7%

profile of v5, /device:TPU:1, one launch (start us, length us, event | category | flops | bytes accessed | tf_op | source)
XLA Modules:
  0.0 144.9 jit_solution(13550648842758287153)
XLA Ops:
  0.8 0.6 add_subtract_fusion.half
  1.3 0.0 copy-start.7
  1.3 0.0 copy-start.2
  1.4 0.0 copy-start.3
  1.4 4.9 %shard_map.84 = (f32[8,96,256]{2,1,0:T(8,128)}, f32[8,96,256]{2,1,0:T(8,128)}, f32[8,64,256]{2,1,0:T(8,128)}) custom-call(s32[3]{0:T(128)} %add_subtract_fusion.half, bf16[896,256]{1,0:T(8,128)(2,1)} %test.5, bf16[2048,896]{1,0:T(8,128)(2,1)} %x_short.5, bf16[2048,896]{1,0:T(8,128)(2,1)} %x_short.5, bf16[2048,896]{1,0:T(8,128)(2,1)} %y_short.5, ...), custom_call_target="tpu_custom_call" | custom-call | tf_op jit(solution)/shard_map/pallas_call | solution.py:328
  6.3 3.3 %collective-permute-start = (f32[8,96,256]{2,1,0:T(8,128)}, f32[8,96,256]{2,1,0:T(8,128)S(1)}, u32[]{:S(2)}, u32[]{:S(2)}) collective-permute-start(f32[8,96,256]{2,1,0:T(8,128)} %get-tuple-element.44), channel_id=1, source_target_pairs={{0,96},{2,98},{4,100},{6,102},{8,104},{10,106},{12,108},{14,110},{... | collective-permute-start | bytes 2359304 | tf_op jit(solution)/shard_map/ppermute | solution.py:452
  9.6 2.7 %collective-permute-start.1 = (f32[8,96,256]{2,1,0:T(8,128)}, f32[8,96,256]{2,1,0:T(8,128)S(1)}, u32[]{:S(2)}, u32[]{:S(2)}) collective-permute-start(f32[8,96,256]{2,1,0:T(8,128)} %get-tuple-element.45), channel_id=1, source_target_pairs={{0,6},{2,4},{4,2},{6,0},{8,14},{10,12},{12,10},{14,8},{16,22},{18,... | collective-permute-start | bytes 2359304 | tf_op jit(solution)/shard_map/ppermute | solution.py:452
  12.3 3.8 %collective-permute-start.2 = (f32[8,64,256]{2,1,0:T(8,128)}, f32[8,64,256]{2,1,0:T(8,128)}, u32[]{:S(2)}, u32[]{:S(2)}) collective-permute-start(f32[8,64,256]{2,1,0:T(8,128)} %get-tuple-element.46), channel_id=1, source_target_pairs={{0,24},{2,26},{4,28},{6,30},{8,16},{10,18},{12,20},{14,22},{16,8},... | collective-permute-start | bytes 1572872 | tf_op jit(solution)/shard_map/ppermute | solution.py:452
  16.1 0.0 copy-done.7
  16.1 0.0 copy-done.2
  16.1 0.0 copy-done.3
  16.1 0.0 copy-start
  16.1 2.0 %copy-done = bf16[2048,896]{1,0:T(8,128)(2,1)S(1)} copy-done((bf16[2048,896]{1,0:T(8,128)(2,1)S(1)}, bf16[2048,896]{1,0:T(8,128)(2,1)}, u32[]{:S(2)}) %copy-start) | copy-done | bytes 3670040
  18.1 0.0 copy-start.1
  18.1 2.0 %copy-done.1 = bf16[2048,896]{1,0:T(8,128)(2,1)S(1)} copy-done((bf16[2048,896]{1,0:T(8,128)(2,1)S(1)}, bf16[2048,896]{1,0:T(8,128)(2,1)}, u32[]{:S(2)}) %copy-start.1) | copy-done | bytes 3670040
  20.2 3.6 %shard_map.85 = (bf16[64,32,256]{2,1,0:T(8,128)(2,1)}, f32[32,256]{1,0:T(8,128)S(1)}) custom-call(s32[1,32]{1,0:T(1,128)S(1)} %copy-done.3, f32[1,896]{1,0:T(1,128)S(1)} %reshape.21.energy_row, bf16[896,256]{1,0:T(8,128)(2,1)S(1)} %copy-done.2, bf16[2048,896]{1,0:T(8,128)(2,1)S(1)} %copy-done, bf16[2048,896]{1,0:T(8,128)(2,1)S(1)} %copy-done, ...), custom_call_target="tpu_custom_call" | custom-call | tf_op jit(solution)/shard_map/pallas_call | solution.py:391
  23.8 0.6 concatenate.10.half
  24.4 4.7 %all-to-all-start = ((bf16[64,32,256]{2,1,0:T(8,128)(2,1)}), bf16[64,32,256]{2,1,0:T(8,128)(2,1)S(1)}, u32[]{:S(2)}, u32[]{:S(2)}) async-start(bf16[64,32,256]{2,1,0:T(8,128)(2,1)} %get-tuple-element.56), calls=%async_computation | async-start | bytes 2097152 | tf_op jit(solution)/shard_map/all_to_all | solution.py:456
  29.1 0.0 collective-permute-done.2.refs_2_
  29.1 0.0 collective-permute-done.refs_0_
  29.1 0.0 copy-start.4
  29.1 0.1 collective-permute-done.1.refs_1_
  29.2 0.8 copy-done.4
  30.0 0.0 copy-start.5
  30.0 0.9 copy-done.5
  30.9 5.8 %shard_map.86 = (f32[4,96,256]{2,1,0:T(8,128)}, f32[4,96,256]{2,1,0:T(8,128)}, f32[4,64,256]{2,1,0:T(8,128)}, f32[4,96,256]{2,1,0:T(8,128)}, f32[4,96,256]{2,1,0:T(8,128)}, /*index=5*/f32[4,64,256]{2,1,0:T(8,128)}) custom-call(s32[6]{0:T(128)} %concatenate.10.half, bf16[896,256]{1,0:T(8,128)(2,1)} %test.5, bf16[2048,896]{1,0:T(8,128)(2,1)} %x_short.5, ...), custom_call_target="tpu_custom_call" | custom-call | tf_op jit(solution)/shard_map/pallas_call | solution.py:328
  36.7 1.0 collective-permute-start.5
  37.7 1.3 collective-permute-start.3
  39.0 1.2 collective-permute-start.4
  40.2 10.6 %collective-permute-done.4 = f32[4,64,256]{2,1,0:T(8,128)S(1)} collective-permute-done((f32[4,64,256]{2,1,0:T(8,128)}, f32[4,64,256]{2,1,0:T(8,128)S(1)}, u32[]{:S(2)}, u32[]{:S(2)}) %collective-permute-start.4) | collective-permute-done | bytes 262176 | tf_op jit(solution)/shard_map/ppermute | solution.py:458
  50.8 1.0 add.91
  51.8 0.0 collective-permute-done.5
  51.8 1.0 add.94
  52.8 0.0 collective-permute-done.3
  52.9 1.0 add.90
  54.0 0.0 all-to-all-done
  54.0 0.6 collective-permute-start.7
  54.6 2.0 %collective-permute-start.6 = (f32[2,160,256]{2,1,0:T(8,128)S(1)}, f32[2,160,256]{2,1,0:T(8,128)S(1)}, u32[]{:S(2)}, u32[]{:S(2)}) collective-permute-start(f32[2,160,256]{2,1,0:T(8,128)S(1)} %fusion), channel_id=1, source_target_pairs={{0,6},{2,4},{4,2},{6,0},{8,14},{10,12},{12,10},{14,8},{16,22},{18,... | collective-permute-start | bytes 983048 | tf_op jit(solution)/shard_map/ppermute | solution.py:477
  56.5 4.7 %collective-permute-done.7 = f32[2,96,256]{2,1,0:T(8,128)S(1)} collective-permute-done((f32[2,96,256]{2,1,0:T(8,128)S(1)}, f32[2,96,256]{2,1,0:T(8,128)S(1)}, u32[]{:S(2)}, u32[]{:S(2)}) %collective-permute-start.7) | collective-permute-done | bytes 196640 | tf_op jit(solution)/shard_map/ppermute | solution.py:477
  61.3 2.2 %collective-permute-done.6 = f32[2,160,256]{2,1,0:T(8,128)S(1)} collective-permute-done((f32[2,160,256]{2,1,0:T(8,128)S(1)}, f32[2,160,256]{2,1,0:T(8,128)S(1)}, u32[]{:S(2)}, u32[]{:S(2)}) %collective-permute-start.6) | collective-permute-done | bytes 327712 | tf_op jit(solution)/shard_map/ppermute | solution.py:477
  63.6 0.6 collective-permute-start.9
  64.2 0.1 constant_dynamic-slice_fusion.1
  64.3 2.6 %collective-permute-start.11 = (bf16[64,16,256]{2,1,0:T(8,128)(2,1)S(1)}, bf16[64,16,256]{2,1,0:T(8,128)(2,1)S(1)}, u32[]{:S(2)}, u32[]{:S(2)}) collective-permute-start(bf16[64,16,256]{2,1,0:T(8,128)(2,1)S(1)} %get-tuple-element.70), channel_id=1, source_target_pairs={{0,1},{1,0},{2,3},{3,2},{4,5},{5,4},{6,7},{7,6},{8,9},{9,8},{10,11... | collective-permute-start | bytes 1572872 | tf_op jit(solution)/shard_map/ppermute | solution.py:473
  66.9 0.0 collective-permute-start.8
  66.9 0.2 collective-permute-done.9
  67.2 5.5 %collective-permute-done.8 = f32[1,160,256]{2,1,0:T(8,128)S(1)} collective-permute-done((f32[1,160,256]{2,1,0:T(8,128)S(1)}, f32[1,160,256]{2,1,0:T(8,128)S(1)}, u32[]{:S(2)}, u32[]{:S(2)}) %collective-permute-start.8) | collective-permute-done | bytes 163872 | tf_op jit(solution)/shard_map/ppermute | solution.py:477
  72.7 1.0 collective-permute-start.10
  73.7 0.0 collective-permute-done.11.other_rows
  73.7 1.2 collective-permute-done.10.away
  74.8 1.0 shard_map.87
  75.8 25.9 %all_to_all.15 = f32[64,16,256]{2,1,0:T(8,128)S(1)} all-to-all(f32[64,16,256]{2,1,0:T(8,128)S(1)} %shard_map.87), channel_id=1, replica_groups=mesh['col'=64,'pw'=2] {'col'}, dimensions={0} | all-to-all | bytes 2097152 | tf_op jit(solution)/shard_map/all_to_all | solution.py:483
  101.7 0.1 reduce_sum.9
  101.8 0.0 copy-start.6
  101.8 0.1 broadcast_in_dim.2
  101.9 21.6 %all_to_all.16 = f32[64,16,256]{2,1,0:T(8,128)S(1)} all-to-all(f32[64,16,256]{2,1,0:T(8,128)S(1)} %broadcast_in_dim.2), channel_id=1, replica_groups=mesh['col'=64,'pw'=2] {'col'}, dimensions={0} | all-to-all | bytes 2097152 | tf_op jit(solution)/shard_map/all_to_all | solution.py:486
  123.6 3.3 %collective-permute-start.12 = (f32[64,16,256]{2,1,0:T(8,128)S(1)}, f32[64,16,256]{2,1,0:T(8,128)S(1)}, u32[]{:S(2)}, u32[]{:S(2)}) collective-permute-start(f32[64,16,256]{2,1,0:T(8,128)S(1)} %all_to_all.16), channel_id=1, source_target_pairs={{0,1},{1,0},{2,3},{3,2},{4,5},{5,4},{6,7},{7,6},{8,9},{9,8},{10,11... | collective-permute-start | bytes 3145736 | tf_op jit(solution)/shard_map/ppermute | solution.py:487
  126.9 0.8 shard_map.88.mine_gram
  127.7 1.5 %collective-permute-done.12 = f32[64,16,256]{2,1,0:T(8,128)S(1)} collective-permute-done((f32[64,16,256]{2,1,0:T(8,128)S(1)}, f32[64,16,256]{2,1,0:T(8,128)S(1)}, u32[]{:S(2)}, u32[]{:S(2)}) %collective-permute-start.12) | collective-permute-done | bytes 1048608 | tf_op jit(solution)/shard_map/ppermute | solution.py:487
  129.1 15.7 %shard_map.89 = (f32[16,256]{1,0:T(8,128)}, f32[256,256]{1,0:T(8,128)}, f32[256,256]{1,0:T(8,128)}) custom-call(s32[1]{0:T(128)} %bitcast.8.where_ref, f32[1024,256]{1,0:T(8,128)S(1)} %bitcast.12, f32[1024,256]{1,0:T(8,128)S(1)} %bitcast.14, f32[256,256]{1,0:T(8,128)S(1)} %shard_map.88.mine_gram), custom_call_target="tpu_custom_call" | custom-call | tf_op jit(solution)/shard_map/pallas_call | solution.py:228
  144.9 0.0 copy-done.6
  (12 shorter events, 0.2 us)
Async XLA Ops:
  1.3 14.7 %copy-start.7 = (f32[896]{0:T(1024)S(1)}, f32[896]{0:T(1024)}, u32[]{:S(2)}) copy-start(f32[896]{0:T(1024)} %param.8) | copy-start | bytes 10756
  1.3 14.7 %copy-start.2 = (bf16[896,256]{1,0:T(8,128)(2,1)S(1)}, bf16[896,256]{1,0:T(8,128)(2,1)}, u32[]{:S(2)}) copy-start(bf16[896,256]{1,0:T(8,128)(2,1)} %test.5) | copy-start | bytes 1376260
  1.4 14.7 %copy-start.3 = (s32[1,32]{1,0:T(1,128)S(1)}, s32[1,32]{1,0:T(1,128)}, u32[]{:S(2)}) copy-start(s32[1,32]{1,0:T(1,128)} %picks_row) | copy-start | bytes 388
  6.3 22.8 %collective-permute-start = (f32[8,96,256]{2,1,0:T(8,128)}, f32[8,96,256]{2,1,0:T(8,128)S(1)}, u32[]{:S(2)}, u32[]{:S(2)}) collective-permute-start(f32[8,96,256]{2,1,0:T(8,128)} %get-tuple-element.44), channel_id=1, source_target_pairs={{0,96},{2,98},{4,100},{6,102},{8,104},{10,106},{12,108},{14,110},{... | collective-permute-start | bytes 2359304 | tf_op jit(solution)/shard_map/ppermute | solution.py:452
  9.6 19.6 %collective-permute-start.1 = (f32[8,96,256]{2,1,0:T(8,128)}, f32[8,96,256]{2,1,0:T(8,128)S(1)}, u32[]{:S(2)}, u32[]{:S(2)}) collective-permute-start(f32[8,96,256]{2,1,0:T(8,128)} %get-tuple-element.45), channel_id=1, source_target_pairs={{0,6},{2,4},{4,2},{6,0},{8,14},{10,12},{12,10},{14,8},{16,22},{18,... | collective-permute-start | bytes 2359304 | tf_op jit(solution)/shard_map/ppermute | solution.py:452
  12.3 16.8 %collective-permute-start.2 = (f32[8,64,256]{2,1,0:T(8,128)}, f32[8,64,256]{2,1,0:T(8,128)}, u32[]{:S(2)}, u32[]{:S(2)}) collective-permute-start(f32[8,64,256]{2,1,0:T(8,128)} %get-tuple-element.46), channel_id=1, source_target_pairs={{0,24},{2,26},{4,28},{6,30},{8,16},{10,18},{12,20},{14,22},{16,8},... | collective-permute-start | bytes 1572872 | tf_op jit(solution)/shard_map/ppermute | solution.py:452
  16.1 2.0 %copy-start = (bf16[2048,896]{1,0:T(8,128)(2,1)S(1)}, bf16[2048,896]{1,0:T(8,128)(2,1)}, u32[]{:S(2)}) copy-start(bf16[2048,896]{1,0:T(8,128)(2,1)} %x_short.5) | copy-start | bytes 11010052
  18.1 2.0 %copy-start.1 = (bf16[2048,896]{1,0:T(8,128)(2,1)S(1)}, bf16[2048,896]{1,0:T(8,128)(2,1)}, u32[]{:S(2)}) copy-start(bf16[2048,896]{1,0:T(8,128)(2,1)} %y_short.5) | copy-start | bytes 11010052
  24.4 29.5 %all-to-all-start = ((bf16[64,32,256]{2,1,0:T(8,128)(2,1)}), bf16[64,32,256]{2,1,0:T(8,128)(2,1)S(1)}, u32[]{:S(2)}, u32[]{:S(2)}) async-start(bf16[64,32,256]{2,1,0:T(8,128)(2,1)} %get-tuple-element.56), calls=%async_computation | async-start | bytes 2097152 | tf_op jit(solution)/shard_map/all_to_all | solution.py:456
  29.1 0.9 copy-start.4
  30.0 0.9 copy-start.5
  36.7 15.1 %collective-permute-start.5 = (f32[4,96,256]{2,1,0:T(8,128)}, f32[4,96,256]{2,1,0:T(8,128)S(1)}, u32[]{:S(2)}, u32[]{:S(2)}) collective-permute-start(f32[4,96,256]{2,1,0:T(8,128)} %get-tuple-element.55), channel_id=1, source_target_pairs={{0,2},{2,0},{4,6},{6,4},{8,10},{10,8},{12,14},{14,12},{16,18},{18,... | collective-permute-start | bytes 1179656 | tf_op jit(solution)/shard_map/ppermute | solution.py:458
  37.7 15.2 %collective-permute-start.3 = (f32[4,96,256]{2,1,0:T(8,128)}, f32[4,96,256]{2,1,0:T(8,128)S(1)}, u32[]{:S(2)}, u32[]{:S(2)}) collective-permute-start(f32[4,96,256]{2,1,0:T(8,128)} %get-tuple-element.51), channel_id=1, source_target_pairs={{0,32},{2,34},{4,36},{6,38},{8,40},{10,42},{12,44},{14,46},{16,48}... | collective-permute-start | bytes 1179656 | tf_op jit(solution)/shard_map/ppermute | solution.py:458
  39.0 11.8 %collective-permute-start.4 = (f32[4,64,256]{2,1,0:T(8,128)}, f32[4,64,256]{2,1,0:T(8,128)S(1)}, u32[]{:S(2)}, u32[]{:S(2)}) collective-permute-start(f32[4,64,256]{2,1,0:T(8,128)} %get-tuple-element.53), channel_id=1, source_target_pairs={{0,8},{2,10},{4,12},{6,14},{8,0},{10,2},{12,4},{14,6},{16,24},{18,... | collective-permute-start | bytes 786440 | tf_op jit(solution)/shard_map/ppermute | solution.py:458
  54.0 7.3 %collective-permute-start.7 = (f32[2,96,256]{2,1,0:T(8,128)S(1)}, f32[2,96,256]{2,1,0:T(8,128)S(1)}, u32[]{:S(2)}, u32[]{:S(2)}) collective-permute-start(f32[2,96,256]{2,1,0:T(8,128)S(1)} %constant_dynamic-slice_fusion.5), channel_id=1, source_target_pairs={{0,96},{2,98},{4,100},{6,102},{8,104},{10,106},{12,108},{14,110},{... | collective-permute-start | bytes 589832 | tf_op jit(solution)/shard_map/ppermute | solution.py:477
  54.6 8.9 %collective-permute-start.6 = (f32[2,160,256]{2,1,0:T(8,128)S(1)}, f32[2,160,256]{2,1,0:T(8,128)S(1)}, u32[]{:S(2)}, u32[]{:S(2)}) collective-permute-start(f32[2,160,256]{2,1,0:T(8,128)S(1)} %fusion), channel_id=1, source_target_pairs={{0,6},{2,4},{4,2},{6,0},{8,14},{10,12},{12,10},{14,8},{16,22},{18,... | collective-permute-start | bytes 983048 | tf_op jit(solution)/shard_map/ppermute | solution.py:477
  63.6 3.5 %collective-permute-start.9 = (f32[1,96,256]{2,1,0:T(8,128)S(1)}, f32[1,96,256]{2,1,0:T(8,128)S(1)}, u32[]{:S(2)}, u32[]{:S(2)}) collective-permute-start(f32[1,96,256]{2,1,0:T(8,128)S(1)} %constant_dynamic-slice_fusion.3), channel_id=1, source_target_pairs={{0,32},{2,34},{4,36},{6,38},{8,40},{10,42},{12,44},{14,46},{16,48}... | collective-permute-start | bytes 294920 | tf_op jit(solution)/shard_map/ppermute | solution.py:477
  64.3 9.4 %collective-permute-start.11 = (bf16[64,16,256]{2,1,0:T(8,128)(2,1)S(1)}, bf16[64,16,256]{2,1,0:T(8,128)(2,1)S(1)}, u32[]{:S(2)}, u32[]{:S(2)}) collective-permute-start(bf16[64,16,256]{2,1,0:T(8,128)(2,1)S(1)} %get-tuple-element.70), channel_id=1, source_target_pairs={{0,1},{1,0},{2,3},{3,2},{4,5},{5,4},{6,7},{7,6},{8,9},{9,8},{10,11... | collective-permute-start | bytes 1572872 | tf_op jit(solution)/shard_map/ppermute | solution.py:473
  66.9 5.8 %collective-permute-start.8 = (f32[1,160,256]{2,1,0:T(8,128)S(1)}, f32[1,160,256]{2,1,0:T(8,128)S(1)}, u32[]{:S(2)}, u32[]{:S(2)}) collective-permute-start(f32[1,160,256]{2,1,0:T(8,128)S(1)} %constant_dynamic-slice_fusion.4), channel_id=1, source_target_pairs={{0,2},{2,0},{4,6},{6,4},{8,10},{10,8},{12,14},{14,12},{16,18},{18,... | collective-permute-start | bytes 491528 | tf_op jit(solution)/shard_map/ppermute | solution.py:477
  72.7 2.1 %collective-permute-start.10 = (f32[256,256]{1,0:T(8,128)S(1)}, f32[256,256]{1,0:T(8,128)S(1)}, u32[]{:S(2)}, u32[]{:S(2)}) collective-permute-start(f32[256,256]{1,0:T(8,128)S(1)} %pad_maximum_fusion), channel_id=1, source_target_pairs={{0,1},{1,0},{2,3},{3,2},{4,5},{5,4},{6,7},{7,6},{8,9},{9,8},{10,11... | collective-permute-start | bytes 786440 | tf_op jit(solution)/shard_map/ppermute | solution.py:478
  101.8 43.1 %copy-start.6 = (f32[16,256]{1,0:T(8,128)}, f32[16,256]{1,0:T(8,128)S(1)}, u32[]{:S(2)}) copy-start(f32[16,256]{1,0:T(8,128)S(1)} %add.107) | copy-start | bytes 49156
  123.6 5.6 %collective-permute-start.12 = (f32[64,16,256]{2,1,0:T(8,128)S(1)}, f32[64,16,256]{2,1,0:T(8,128)S(1)}, u32[]{:S(2)}, u32[]{:S(2)}) collective-permute-start(f32[64,16,256]{2,1,0:T(8,128)S(1)} %all_to_all.16), channel_id=1, source_target_pairs={{0,1},{1,0},{2,3},{3,2},{4,5},{5,4},{6,7},{7,6},{8,9},{9,8},{10,11... | collective-permute-start | bytes 3145736 | tf_op jit(solution)/shard_map/ppermute | solution.py:487
